TPU v7x, 32 devices: a whole 2x2x4 slice. The times are simulated.
32 devices in a mesh: groups: 2 (over y), patch: 8 (over z, x), member: 2 (over core).
Axes of the slice: x: 2, y: 2, z: 4, core: 2. Of those that a mesh axis runs over, the one named last changes fastest.
Arguments:
- fields: bfloat16 [8, 16384, 84], P(('groups', 'member'), 'patch'), parts along dimension 0, may hold values from -6 to 6
- w_embed: bfloat16 [84, 512], replicated, may hold values from -0.625 to 0.625
- b_embed: float32 [512], replicated, may hold values from -3 to 3
- w_encode: bfloat16 [512, 512], replicated, may hold values from -0.25 to 0.25
- b_encode: float32 [512], replicated, may hold values from -3 to 3
- mesh_gain: float32 [512], replicated, may hold values from 0.1 to 1.9
- w_receive: bfloat16 [512, 512], replicated, may hold values from -0.25 to 0.25
- w_sender: bfloat16 [512, 512], replicated, may hold values from -0.25 to 0.25
- b_process: float32 [512], replicated, may hold values from -3 to 3
- w_update: bfloat16 [512, 512], replicated, may hold values from -0.25 to 0.25
- w_decmesh: bfloat16 [512, 512], replicated, may hold values from -0.25 to 0.25
- w_decgrid: bfloat16 [512, 512], replicated, may hold values from -0.25 to 0.25
- b_decode: float32 [512], replicated, may hold values from -3 to 3
- w_output: bfloat16 [512, 84], replicated, may hold values from -0.25 to 0.25
- b_output: float32 [84], replicated, may hold values from -3 to 3
- g2m_senders: int32 [2048, 16], P('patch'), may hold values from -1 to 16383, as said below
- m2g_senders: int32 [16384, 3], P('patch'), may hold values from 0 to 2047, as said below
- mesh_neighbours: int32 [2048, 6], P('patch'), may hold values from 0 to 2047, as said below
- climatology: bfloat16 [16384, 84], P('patch'), may hold values from -6 to 6
- week_sum: float32 [32768, 84], P(('groups', 'patch')), parts along dimension 0, may hold values from -6 to 6
Outputs:
- prediction: bfloat16 [8, 16384, 84], P(('groups', 'member'), 'patch'), parts along dimension 0
- week_total: float32 [32768, 84], P(('groups', 'patch')), parts along dimension 0
There are 2 independent parts, one for each index of `groups`. A program takes and returns all parts, laid end to end along the dimension named above; an argument that names none is the same for every part. Nothing has to cross between parts.
Inputs may be any that keep to these rules, and one draw needn't show every extreme that they name: `g2m_senders`: for mesh node n = p * 256 + r (0 <= r < 256) every used slot holds (p * 2048 + r * 8 + k) modulo 16384 with -128 <= k <= 135; both ends of k occur in every draw. Used slots come first, -1 marks empty ones; a mesh node has 8 to 16 used slots, and some mesh node has all 16 in every draw. `m2g_senders`: for grid node g = p * 2048 + r (0 <= r < 2048) every entry is (p * 256 + r // 8 + k) modulo 2048 with -32 <= k <= 32; both ends of k occur in every draw. `mesh_neighbours`: every neighbour of mesh node n is (n + k) modulo 2048 with 1 <= |k| <= 32; both k = 32 and k = -32 occur in every draw.
All inputs are finite; a program needn't handle non-finite values.
Results may differ from a plain program's by a relative error of at most 0.008.
Values may be sent and summed in bfloat16 or wider, within the bound.
No kernel may reach another device: no remote copies, remote signals or barrier semaphores. Data moves between devices by JAX's collectives and lax.ppermute only.
A program may use at most 128 MiB of HBM per device.

v0:
```python
import jax
import jax.numpy as jnp
from jax import lax
from jax.sharding import PartitionSpec as P

TRI = 3
NBRS = 6
REACH = 32
GRIM = 128


def extended_2(block, sides, width):
    for axis, dim in sides:
        count = lax.axis_size(axis)
        forward = [(i, i + 1) for i in range(count - 1)]
        forward.append((count - 1, 0))
        backward = [(target, source) for source, target in forward]
        low = lax.ppermute(
            lax.slice_in_dim(block, block.shape[dim] - width, None, axis=dim), axis, forward
        )
        high = lax.ppermute(lax.slice_in_dim(block, 0, width, axis=dim), axis, backward)
        block = jnp.concatenate([low, block, high], axis=dim)
    return block


def rounded(values):
    return lax.optimization_barrier(values.astype(jnp.bfloat16)).astype(jnp.float32)


def shards(
    fields,
    w_embed,
    b_embed,
    w_encode,
    b_encode,
    mesh_gain,
    w_receive,
    w_sender,
    b_process,
    w_update,
    w_decmesh,
    w_decgrid,
    b_decode,
    w_output,
    b_output,
    g2m_senders,
    m2g_senders,
    mesh_neighbours,
    climatology,
    week_sum,
):
    members, grid_rows, channels = fields.shape
    hidden = w_encode.shape[0]
    mesh_rows = mesh_neighbours.shape[0]
    slots = g2m_senders.shape[1]
    patches = lax.axis_size("patch")
    position = lax.axis_index("patch")
    flat_rows = fields.reshape(-1, channels)
    latent = jax.nn.silu(jnp.dot(flat_rows, w_embed, preferred_element_type=jnp.float32) + b_embed)
    grid_latent = latent.astype(jnp.bfloat16).reshape(members, -1, hidden)
    flat_rows = grid_latent.reshape(-1, hidden)
    message = jax.nn.silu(
        jnp.dot(flat_rows, w_encode, preferred_element_type=jnp.float32) + b_encode
    )
    messages = message.astype(jnp.bfloat16).reshape(members, -1, hidden)
    ext_messages = extended_2(messages, (("patch", 1),), GRIM)
    first_grid = position * grid_rows - GRIM
    valid = g2m_senders >= 0
    enc_local = jnp.where(valid, jnp.mod(g2m_senders - first_grid, grid_rows * patches), 0)
    gathered = jnp.take(ext_messages, enc_local.reshape(-1), axis=1).reshape(
        members, mesh_rows, slots, hidden
    )
    gathered = jnp.where(valid[None, :, :, None], gathered, jnp.zeros_like(gathered))
    mesh_sum = jnp.sum(gathered.astype(jnp.float32), axis=2)
    scale = lax.rsqrt(jnp.mean(mesh_sum * mesh_sum, axis=-1, keepdims=True) + 1e-05)
    mesh_latent = (mesh_gain * mesh_sum * scale).astype(jnp.bfloat16)
    extended = extended_2(mesh_latent, (("patch", 1),), REACH)
    ext_rows = extended.shape[1]
    first_node = position * mesh_rows - REACH
    local_neighbours = jnp.mod(mesh_neighbours - first_node, mesh_rows * patches)
    sender_part = jnp.dot(
        extended.reshape(members * ext_rows, hidden), w_sender, preferred_element_type=jnp.float32
    )
    sender_part = sender_part.reshape(members, ext_rows, hidden)
    receiver_part = jnp.dot(
        mesh_latent.reshape(members * mesh_rows, hidden),
        w_receive,
        preferred_element_type=jnp.float32,
    )
    receiver_part = receiver_part.reshape(members, mesh_rows, hidden) + b_process
    process_total = jnp.zeros((members, mesh_rows, hidden), jnp.float32)
    for column in range(NBRS):
        process_total = process_total + jax.nn.silu(
            receiver_part + jnp.take(sender_part, local_neighbours[:, column], axis=1)
        )
    process_sum = process_total.astype(jnp.bfloat16).reshape(members * mesh_rows, hidden)
    update = jnp.dot(process_sum, w_update, preferred_element_type=jnp.float32).reshape(
        members, mesh_rows, hidden
    )
    mesh_new = (mesh_latent.astype(jnp.float32) + update).astype(jnp.bfloat16)
    ext_new = extended_2(mesh_new, (("patch", 1),), REACH)
    mesh_part = jnp.dot(
        ext_new.reshape(members * ext_rows, hidden), w_decmesh, preferred_element_type=jnp.float32
    )
    mesh_part = mesh_part.reshape(members, ext_rows, hidden)
    dec_local = jnp.mod(m2g_senders - first_node, mesh_rows * patches)
    grid_part = jnp.dot(
        grid_latent.reshape(members * grid_rows, hidden),
        w_decgrid,
        preferred_element_type=jnp.float32,
    )
    grid_part = grid_part.reshape(members, grid_rows, hidden) + b_decode
    decoded = jnp.zeros((members, grid_rows, hidden), jnp.float32)
    for column in range(TRI):
        decoded = decoded + rounded(
            jax.nn.silu(jnp.take(mesh_part, dec_local[:, column], axis=1) + grid_part)
        )
    grid_sum = decoded.astype(jnp.bfloat16)
    delta = (
        jnp.dot(
            grid_sum.reshape(members * grid_rows, hidden),
            w_output,
            preferred_element_type=jnp.float32,
        )
        + b_output
    )
    flat_fields = fields.reshape(members * grid_rows, channels)
    prediction = (
        (flat_fields.astype(jnp.float32) + delta)
        .astype(jnp.bfloat16)
        .reshape(members, grid_rows, channels)
    )
    local_total = jnp.sum(prediction.astype(jnp.float32), axis=0)
    ensemble = lax.psum(local_total.astype(jnp.bfloat16), "member").astype(jnp.float32) / (
        members * lax.axis_size("member")
    )
    week_total = week_sum + ensemble - climatology.astype(jnp.float32)
    return (prediction, week_total)


def solution(mesh):
    placed = (
        P(("groups", "member"), "patch", None),
        P(),
        P(),
        P(),
        P(),
        P(),
        P(),
        P(),
        P(),
        P(),
        P(),
        P(),
        P(),
        P(),
        P(),
        P("patch", None),
        P("patch", None),
        P("patch", None),
        P("patch", None),
        P(("groups", "patch"), None),
    )
    return jax.shard_map(
        shards,
        mesh=mesh,
        in_specs=placed,
        out_specs=(P(("groups", "member"), "patch", None), P(("groups", "patch"), None)),
        check_vma=False,
    )
```

profile of v0, /device:TPU:0, one launch (start us, length us, event | category | flops | bytes accessed | tf_op | source)
XLA Modules:
  0.0 296.9 jit_solution(9666564846103333015)
XLA Ops:
  7.2 0.0 copy-start
  7.2 0.0 all-reduce.2.cloned.1.call-start
  7.2 1.7 pad.19
  8.9 0.2 copy.144
  9.2 0.0 copy-start.16
  9.2 3.6 %multiply_convert_fusion.4 = bf16[4096,512]{1,0:T(8,128)(2,1)S(1)} fusion(bf16[4096,84]{0,1:T(8,128)(2,1)S(1)} %bitcast.96, bf16[84,512]{1,0:T(8,128)(2,1)} %param.25, f32[512]{0:T(512)} %param.26), kind=kOutput, calls=%fused_computation.24 | convolution fusion | flops 364904448 | bytes 4970496 | tf_op jit(solution)/shard_map/dot_general | solution.py:59
  12.8 3.7 %multiply_convert_fusion.3 = bf16[4096,512]{1,0:T(8,128)(2,1)S(1)} fusion(bf16[4096,512]{1,0:T(8,128)(2,1)S(1)} %multiply_convert_fusion.4, bf16[512,512]{1,0:T(8,128)(2,1)S(1)} %copy-done, f32[512]{0:T(512)S(1)} %copy-done.16), kind=kOutput, calls=%fused_computation.23 | convolution fusion | flops 2160066560 | bytes 8914944 | tf_op jit(solution)/shard_map/dot_general | solution.py:63
  16.5 0.0 copy-start.10
  16.6 0.0 copy-start.8
  16.6 0.0 copy-start.9
  16.6 0.0 copy-start.6
  16.6 16.4 %copy.120 = bf16[2,2048,512]{2,0,1:T(2,128)(2,1)S(1)} copy(bf16[2,2048,512]{2,1,0:T(8,128)(2,1)S(1)} %bitcast.98) | data formatting | bytes 8388608 | tf_op jit(solution)/shard_map/reshape | solution.py:65
  33.0 0.0 copy-start.2
  33.0 2.0 copy-done.2
  35.0 0.4 fusion.43
  35.3 3.0 %collective-permute-start = (bf16[2,128,512]{2,0,1:T(2,128)(2,1)S(1)}, bf16[2,128,512]{2,0,1:T(2,128)(2,1)S(1)}, u32[]{:S(2)}, u32[]{:S(2)}) collective-permute-start(bf16[2,128,512]{2,0,1:T(2,128)(2,1)S(1)} %get-tuple-element.9), channel_id=1, source_target_pairs={{0,2},{2,4},{4,6},{6,8},{8,10},{10,12},{12,14},{14,0},{1,3},{3,5},... | collective-permute-start | bytes 786440 | tf_op jit(solution)/shard_map/ppermute | solution.py:18
  38.3 3.1 %collective-permute-start.1 = (bf16[2,128,512]{2,0,1:T(2,128)(2,1)S(1)}, bf16[2,128,512]{2,0,1:T(2,128)(2,1)S(1)}, u32[]{:S(2)}, u32[]{:S(2)}) collective-permute-start(bf16[2,128,512]{2,0,1:T(2,128)(2,1)S(1)} %get-tuple-element.10), channel_id=1, source_target_pairs={{2,0},{4,2},{6,4},{8,6},{10,8},{12,10},{14,12},{0,14},{3,1},{5,3},... | collective-permute-start | bytes 786440 | tf_op jit(solution)/shard_map/ppermute | solution.py:21
  41.8 0.1 copy.123
  41.9 0.1 reshape.114
  42.1 7.8 %fusion.48 = f32[4096,512]{1,0:T(8,128)} fusion(bf16[4096,512]{1,0:T(8,128)(2,1)} %copy-done.3, bf16[512,512]{1,0:T(8,128)(2,1)S(1)} %copy-done.6), kind=kOutput, calls=%fused_computation.130 | convolution fusion | flops 2147483648 | bytes 13107200 | tf_op jit(solution)/shard_map/dot_general | solution.py:107
  49.9 0.1 copy.119
  50.0 0.1 copy.118
  50.2 0.0 collective-permute-done
  50.2 1.5 collective-permute-done.1
  51.7 17.8 %pad_maximum_fusion = bf16[2,2304,512]{2,0,1:T(2,128)(2,1)} fusion(bf16[2,128,512]{2,0,1:T(2,128)(2,1)S(1)} %collective-permute-done.1, bf16[2,2048,512]{2,0,1:T(2,128)(2,1)} %copy-done.2, bf16[2,128,512]{2,0,1:T(2,128)(2,1)S(1)} %collective-permute-done), kind=kLoop, calls=%fused_computation.27 | loop fusion | flops 4718592 | bytes 9437184 | tf_op jit(solution)/shard_map/concatenate | solution.py:22
  69.6 44.7 %gather_fusion = bf16[4096,2,512]{2,1,0:T(2,128)(2,1)} fusion(bf16[2,2304,512]{2,0,1:T(2,128)(2,1)} %pad_maximum_fusion, s32[4096]{0:T(1024)S(1)} %broadcast_clamp_fusion), kind=kCustom, calls=%fused_computation.9 | custom fusion | bytes 16793600 | tf_op jit(solution)/shard_map/jit(_take)/gather | solution.py:70
  114.3 17.4 %convert_reduce_fusion = f32[2,256,512]{2,0,1:T(2,128)S(1)} fusion(pred[256,16]{1,0:T(8,128)(4,1)S(1)} %copy.118, pred[256,16]{1,0:T(8,128)(4,1)S(1)} %copy.119, bf16[4096,2,512]{2,1,0:T(2,128)(2,1)} %gather_fusion), kind=kLoop, calls=%fused_computation.10 | loop fusion | flops 16515072 | bytes 9445376 | tf_op jit(solution)/shard_map/reduce_sum | solution.py:74
  131.6 0.5 multiply_reduce_fusion
  132.1 0.1 copy.125
  132.2 0.2 fusion.4
  132.4 0.3 collective-permute-start.2
  132.8 4.4 %collective-permute-start.3 = (bf16[2,32,512]{2,1,0:T(8,128)(2,1)S(1)}, bf16[2,32,512]{2,1,0:T(8,128)(2,1)S(1)}, u32[]{:S(2)}, u32[]{:S(2)}) collective-permute-start(bf16[2,32,512]{2,1,0:T(8,128)(2,1)S(1)} %get-tuple-element.14), channel_id=1, source_target_pairs={{2,0},{4,2},{6,4},{8,6},{10,8},{12,10},{14,12},{0,14},{3,1},{5,3},... | collective-permute-start | bytes 196616 | tf_op jit(solution)/shard_map/ppermute | solution.py:21
  137.2 2.2 collective-permute-done.2
  139.4 0.0 collective-permute-done.3
  139.4 0.0 copy-done.14
  139.4 0.5 fusion.5
  140.0 1.0 copy.126
  141.0 2.8 gather_fusion.6
  143.7 2.7 gather_fusion.5
  146.4 2.7 gather_fusion.4
  149.1 2.7 gather_fusion.3
  151.8 2.7 gather_fusion.2
  154.5 2.7 gather_fusion.1
  157.2 5.8 %fusion.2 = bf16[2,256,512]{2,1,0:T(8,128)(2,1)S(1)} fusion(f32[256,2,512]{2,1,0:T(2,128)} %gather_fusion.6, f32[256,2,512]{2,1,0:T(2,128)} %gather_fusion.5, f32[256,2,512]{2,1,0:T(2,128)} %gather_fusion.4, f32[256,2,512]{2,1,0:T(2,128)} %gather_fusion.3, f32[256,2,512]{2,1,0:T(2,128)} %gather_fusion.2, f32[256,2,512]{2,1,0:T(2,128)} %gather_fusion.1, ...), kind=kOutput, calls=%fused_computation.31 | convolution fusion | flops 548929536 | bytes 8392192 | tf_op jit(solution)/shard_map/dot_general | solution.py:97
  163.0 1.0 collective-permute-start.4
  164.0 4.1 %collective-permute-start.5 = (bf16[2,32,512]{2,1,0:T(8,128)(2,1)S(1)}, bf16[2,32,512]{2,1,0:T(8,128)(2,1)S(1)}, u32[]{:S(2)}, u32[]{:S(2)}) collective-permute-start(bf16[2,32,512]{2,1,0:T(8,128)(2,1)S(1)} %get-tuple-element.12), channel_id=1, source_target_pairs={{2,0},{4,2},{6,4},{8,6},{10,8},{12,10},{14,12},{0,14},{3,1},{5,3},... | collective-permute-start | bytes 196616 | tf_op jit(solution)/shard_map/ppermute | solution.py:21
  168.1 2.0 collective-permute-done.4
  170.0 0.0 collective-permute-done.5
  170.1 0.0 copy-done.15
  170.1 0.5 fusion.11
  170.6 1.0 copy.138
  171.6 22.8 %gather_fusion.9 = f32[2048,2,512]{2,1,0:T(2,128)} fusion(f32[2,320,512]{2,0,1:T(2,128)S(1)} %copy.138, s32[2048]{0:T(1024)S(1)} %fusion.37), kind=kCustom, calls=%fused_computation.8.clone | custom fusion | bytes 16785408 | tf_op jit(solution)/shard_map/jit(_take)/gather | solution.py:116
  194.4 22.7 %gather_fusion.8 = f32[2048,2,512]{2,1,0:T(2,128)} fusion(f32[2,320,512]{2,0,1:T(2,128)S(1)} %copy.138, s32[2048]{0:T(1024)S(1)} %fusion.36), kind=kCustom, calls=%fused_computation.7.clone | custom fusion | bytes 16785408 | tf_op jit(solution)/shard_map/jit(_take)/gather | solution.py:116
  217.1 22.8 %gather_fusion.7 = f32[2048,2,512]{2,1,0:T(2,128)} fusion(f32[2,320,512]{2,0,1:T(2,128)S(1)} %copy.138, s32[2048]{0:T(1024)S(1)} %fusion.35), kind=kCustom, calls=%fused_computation.1.clone | custom fusion | bytes 16785408 | tf_op jit(solution)/shard_map/jit(_take)/gather | solution.py:116
  239.9 19.2 %multiply_convert_fusion.2 = (bf16[2,2048,512]{2,1,0:T(8,128)(2,1)S(1)}, bf16[2,2048,512]{2,1,0:T(8,128)(2,1)S(1)}, bf16[2,2048,512]{2,1,0:T(8,128)(2,1)}) fusion(f32[2048,2,512]{2,1,0:T(2,128)} %gather_fusion.7, f32[2,2048,512]{2,1,0:T(8,128)} %bitcast.94, f32[512]{0:T(512)S(1)} %copy-done.12, pred[2048]{0:T(1024)(128)(4,1)S(1)} %compare_and_fusion.3, ...), kind=kLoop, calls=%fused_computation.22 | loop fusion | flops 46137344 | bytes 46145536 | tf_op jit(solution)/shard_map/convert_element_type | solution.py:27
  259.1 4.0 %add_convert_fusion = bf16[2,2048,512]{2,1,0:T(8,128)(2,1)S(1)} fusion(bf16[2,2048,512]{2,1,0:T(8,128)(2,1)} %get-tuple-element.8, bf16[2,2048,512]{2,1,0:T(8,128)(2,1)S(1)} %get-tuple-element.7, bf16[2,2048,512]{2,1,0:T(8,128)(2,1)S(1)} %get-tuple-element.6), kind=kLoop, calls=%fused_computation.19 | loop fusion | flops 12582912 | bytes 16777216 | tf_op jit(solution)/shard_map/convert_element_type | solution.py:118
  263.1 0.0 copy-start.5
  263.2 1.4 fusion.1
  264.6 0.4 reshape.117
  265.0 0.0 copy-start.4
  265.0 2.6 reduce_sum.32
  267.6 0.0 all-reduce.2.cloned.1.call-update
  267.6 20.3 %all-reduce.2.cloned.1.call-done = bf16[2048,84]{0,1:T(8,128)(2,1)} async-done(((bf16[2048,84]{0,1:T(8,128)(2,1)}), bf16[2048,84]{0,1:T(8,128)(2,1)}) %all-reduce.2.cloned.1.call-update) | async-done | bytes 344080 | tf_op jit(solution)/shard_map/psum | solution.py:134
  287.9 2.1 convert_subtract_fusion
  (54 shorter events, 0.3 us)
Async XLA Ops:
  7.2 5.6 %copy-start = (bf16[512,512]{1,0:T(8,128)(2,1)S(1)}, bf16[512,512]{1,0:T(8,128)(2,1)}, u32[]{:S(2)}) copy-start(bf16[512,512]{1,0:T(8,128)(2,1)} %param.27) | copy-start | bytes 1572868
  7.2 280.8 %all-reduce.2.cloned.1.call-start = ((), (), s32[]{:S(2)}) async-start(), calls=%async_computation | async-start | bytes 720896 | tf_op jit(solution)/shard_map/psum | solution.py:134
  9.2 3.6 %copy-start.16 = (f32[512]{0:T(512)S(1)}, f32[512]{0:T(512)}, u32[]{:S(2)}) copy-start(f32[512]{0:T(512)} %param.28) | copy-start | bytes 6148
  12.8 3.7 %copy-start.3 = (bf16[4096,512]{1,0:T(8,128)(2,1)}, bf16[4096,512]{1,0:T(8,128)(2,1)S(1)}, u32[]{:S(2)}) copy-start(bf16[4096,512]{1,0:T(8,128)(2,1)S(1)} %multiply_convert_fusion.4) | copy-start | bytes 12582916
  16.5 24.9 %copy-start.10 = (s32[256,6]{0,1:T(8,128)S(1)}, s32[256,6]{0,1:T(8,128)}, u32[]{:S(2)}) copy-start(s32[256,6]{0,1:T(8,128)} %param.41) | copy-start | bytes 18436
  16.6 25.0 %copy-start.8 = (s32[2048,3]{0,1:T(4,128)S(1)}, s32[2048,3]{0,1:T(4,128)}, u32[]{:S(2)}) copy-start(s32[2048,3]{0,1:T(4,128)} %param.40) | copy-start | bytes 73732
  16.6 25.2 %copy-start.9 = (s32[256,16]{0,1:T(8,128)S(1)}, s32[256,16]{0,1:T(8,128)}, u32[]{:S(2)}) copy-start(s32[256,16]{0,1:T(8,128)} %param.39) | copy-start | bytes 49156
  16.6 25.5 %copy-start.6 = (bf16[512,512]{1,0:T(8,128)(2,1)S(1)}, bf16[512,512]{1,0:T(8,128)(2,1)}, u32[]{:S(2)}) copy-start(bf16[512,512]{1,0:T(8,128)(2,1)} %param.35) | copy-start | bytes 1572868
  33.0 2.0 copy-start.2
  35.3 14.8 %collective-permute-start = (bf16[2,128,512]{2,0,1:T(2,128)(2,1)S(1)}, bf16[2,128,512]{2,0,1:T(2,128)(2,1)S(1)}, u32[]{:S(2)}, u32[]{:S(2)}) collective-permute-start(bf16[2,128,512]{2,0,1:T(2,128)(2,1)S(1)} %get-tuple-element.9), channel_id=1, source_target_pairs={{0,2},{2,4},{4,6},{6,8},{8,10},{10,12},{12,14},{14,0},{1,3},{3,5},... | collective-permute-start | bytes 786440 | tf_op jit(solution)/shard_map/ppermute | solution.py:18
  38.3 13.4 %collective-permute-start.1 = (bf16[2,128,512]{2,0,1:T(2,128)(2,1)S(1)}, bf16[2,128,512]{2,0,1:T(2,128)(2,1)S(1)}, u32[]{:S(2)}, u32[]{:S(2)}) collective-permute-start(bf16[2,128,512]{2,0,1:T(2,128)(2,1)S(1)} %get-tuple-element.10), channel_id=1, source_target_pairs={{2,0},{4,2},{6,4},{8,6},{10,8},{12,10},{14,12},{0,14},{3,1},{5,3},... | collective-permute-start | bytes 786440 | tf_op jit(solution)/shard_map/ppermute | solution.py:21
  114.3 17.9 %copy-start.11 = (f32[512]{0:T(512)S(1)}, f32[512]{0:T(512)}, u32[]{:S(2)}) copy-start(f32[512]{0:T(512)} %param.29) | copy-start | bytes 6148
  114.3 25.2 %copy-start.14 = (bf16[512,512]{1,0:T(8,128)(2,1)S(1)}, bf16[512,512]{1,0:T(8,128)(2,1)}, u32[]{:S(2)}) copy-start(bf16[512,512]{1,0:T(8,128)(2,1)} %param.31) | copy-start | bytes 1572868
  132.4 7.0 %collective-permute-start.2 = (bf16[2,32,512]{2,1,0:T(8,128)(2,1)S(1)}, bf16[2,32,512]{2,1,0:T(8,128)(2,1)S(1)}, u32[]{:S(2)}, u32[]{:S(2)}) collective-permute-start(bf16[2,32,512]{2,1,0:T(8,128)(2,1)S(1)} %get-tuple-element.13), channel_id=1, source_target_pairs={{0,2},{2,4},{4,6},{6,8},{8,10},{10,12},{12,14},{14,0},{1,3},{3,5},... | collective-permute-start | bytes 196616 | tf_op jit(solution)/shard_map/ppermute | solution.py:18
  132.8 6.7 %collective-permute-start.3 = (bf16[2,32,512]{2,1,0:T(8,128)(2,1)S(1)}, bf16[2,32,512]{2,1,0:T(8,128)(2,1)S(1)}, u32[]{:S(2)}, u32[]{:S(2)}) collective-permute-start(bf16[2,32,512]{2,1,0:T(8,128)(2,1)S(1)} %get-tuple-element.14), channel_id=1, source_target_pairs={{2,0},{4,2},{6,4},{8,6},{10,8},{12,10},{14,12},{0,14},{3,1},{5,3},... | collective-permute-start | bytes 196616 | tf_op jit(solution)/shard_map/ppermute | solution.py:21
  137.2 20.0 %copy-start.17 = (f32[512]{0:T(512)S(1)}, f32[512]{0:T(512)}, u32[]{:S(2)}) copy-start(f32[512]{0:T(512)} %param.32) | copy-start | bytes 6148
  157.2 12.9 %copy-start.15 = (bf16[512,512]{1,0:T(8,128)(2,1)S(1)}, bf16[512,512]{1,0:T(8,128)(2,1)}, u32[]{:S(2)}) copy-start(bf16[512,512]{1,0:T(8,128)(2,1)} %param.34) | copy-start | bytes 1572868
  163.0 7.0 %collective-permute-start.4 = (bf16[2,32,512]{2,1,0:T(8,128)(2,1)S(1)}, bf16[2,32,512]{2,1,0:T(8,128)(2,1)S(1)}, u32[]{:S(2)}, u32[]{:S(2)}) collective-permute-start(bf16[2,32,512]{2,1,0:T(8,128)(2,1)S(1)} %get-tuple-element.11), channel_id=1, source_target_pairs={{0,2},{2,4},{4,6},{6,8},{8,10},{10,12},{12,14},{14,0},{1,3},{3,5},... | collective-permute-start | bytes 196616 | tf_op jit(solution)/shard_map/ppermute | solution.py:18
  164.0 6.0 %collective-permute-start.5 = (bf16[2,32,512]{2,1,0:T(8,128)(2,1)S(1)}, bf16[2,32,512]{2,1,0:T(8,128)(2,1)S(1)}, u32[]{:S(2)}, u32[]{:S(2)}) collective-permute-start(bf16[2,32,512]{2,1,0:T(8,128)(2,1)S(1)} %get-tuple-element.12), channel_id=1, source_target_pairs={{2,0},{4,2},{6,4},{8,6},{10,8},{12,10},{14,12},{0,14},{3,1},{5,3},... | collective-permute-start | bytes 196616 | tf_op jit(solution)/shard_map/ppermute | solution.py:21
  217.1 22.8 %copy-start.12 = (f32[512]{0:T(512)S(1)}, f32[512]{0:T(512)}, u32[]{:S(2)}) copy-start(f32[512]{0:T(512)} %param.36) | copy-start | bytes 6148
  259.1 4.0 %copy-start.7 = (bf16[512,84]{0,1:T(8,128)(2,1)S(1)}, bf16[512,84]{0,1:T(8,128)(2,1)}, u32[]{:S(2)}) copy-start(bf16[512,84]{0,1:T(8,128)(2,1)} %param.37) | copy-start | bytes 258052
  259.1 4.0 %copy-start.13 = (f32[84]{0:T(128)S(1)}, f32[84]{0:T(128)}, u32[]{:S(2)}) copy-start(f32[84]{0:T(128)} %param.38) | copy-start | bytes 1012
  259.1 30.9 %copy-start.1 = (bf16[512,512]{1,0:T(8,128)(2,1)S(1)}, bf16[512,512]{1,0:T(8,128)(2,1)}, u32[]{:S(2)}) copy-start(bf16[512,512]{1,0:T(8,128)(2,1)} %param.27) | copy-start | bytes 1572868
  263.1 24.8 %copy-start.5 = (f32[2048,84]{0,1:T(8,128)S(1)}, f32[2048,84]{0,1:T(8,128)}, u32[]{:S(2)}) copy-start(f32[2048,84]{0,1:T(8,128)} %param.43) | copy-start | bytes 2064388
  265.0 25.0 %copy-start.4 = (bf16[2,2048,84]{1,0,2:T(2,128)(2,1)}, bf16[2,2048,84]{1,0,2:T(2,128)(2,1)S(1)}, u32[]{:S(2)}) copy-start(bf16[2,2048,84]{1,0,2:T(2,128)(2,1)S(1)} %reshape.117) | copy-start | bytes 2064388
Sparse Core Ops, SparseCore 0:
  267.7 20.1 all-reduce.1
where the time goes:
time: 297 us
  local copies, waits for them, and re-layouts  153 us (52%)
  other arithmetic  64 us (22%)
  waiting for transfers between devices  26.1 us (9%)
  matrix products  23.3 us (8%)
  starting transfers between devices  16 us (5%)
  between operations  14.5 us (5%)
    gather x3, local copies, waits for them, and re-layouts, shards(): jnp.take(mesh_part, dec_local[:, column], axis=1) + grid_part  68.3 us
    gather x1, local copies, waits for them, and re-layouts, shards(): jnp.take(ext_messages, enc_local.reshape(-1), axis=1)  44.7 us
    psum x1, waiting for transfers between devices, shards(): lax.psum(local_total.astype(jnp.bfloat16), 'member').astype(jnp.float32)  20.3 us
    convert_element_type x1, other arithmetic, rounded(): values.astype(jnp.bfloat16)  19.2 us
    concatenate x1, other arithmetic, extended_2(): block = jnp.concatenate([low, block, high], axis=dim)  17.8 us
    reduce_sum x1, other arithmetic, shards(): mesh_sum = jnp.sum(gathered.astype(jnp.float32), axis=2)  17.4 us
    reshape x1, local copies, waits for them, and re-layouts, shards(): messages = message.astype(jnp.bfloat16).reshape(members, -1, hidden)  16.4 us
    gather x6, local copies, waits for them, and re-layouts, shards(): jnp.take(sender_part, local_neighbours[:, column], axis=1)  16.2 us
  transfers between devices with their start and end apart: 7, of which 4 were waited for; matrix products, arithmetic and copies ran while one was open for 3% of the time, Pallas kernels for 0%

commit v1 on v0

v1 whole, which is shorter than its diff:
```python
import functools

import jax
import jax.numpy as jnp
from jax import lax
from jax.experimental import pallas as pl
from jax.experimental.pallas import tpu as pltpu
from jax.sharding import PartitionSpec as P

REACH = 32
GRIM = 128
MHALO = 2 * REACH
EMPTY = -4096
F32 = jnp.float32
BF16 = jnp.bfloat16


def dot(a, b):
    return jnp.dot(a, b, preferred_element_type=F32)


def silu(u):
    return u + u * jnp.tanh(u)


def iota(shape, dim):
    return lax.broadcasted_iota(jnp.int32, shape, dim)


def ranks(shape, dim):
    return iota(shape, dim).astype(F32).astype(BF16)


def twice(a):
    return jnp.concatenate([a, a], axis=0)


def wide(a, width):
    return jnp.concatenate([a] * (width // a.shape[1]), axis=1)


def wrap(a, size):
    a = jnp.where(a < 0, a + size, a)
    return jnp.where(a >= size, a - size, a)


def small(idx):
    return idx.astype(F32).astype(BF16)


def marks(idx, height):
    rows = ranks((height, idx.shape[1]), 0)
    return jnp.where(rows == idx, jnp.ones((), BF16), jnp.zeros((), BF16))


def counts(idx, height, base):
    parts = []
    for first in range(0, height, 256):
        size = min(256, height - first)
        near = small(idx - (base + first))
        total = marks(near[0:1], size)
        for slot in range(1, idx.shape[0]):
            total = total + marks(near[slot : slot + 1], size)
        parts.append(total)
    return parts[0] if len(parts) == 1 else jnp.concatenate(parts, axis=0)


def spread(channels, members, member):
    shape = (channels * members, channels)
    return jnp.where(iota(shape, 0) == iota(shape, 1) * members + member, 1.0, 0.0).astype(BF16)


def turned(w, scale):
    return (w.astype(F32) * scale).T.astype(BF16)


def column(b, scale):
    return (jnp.broadcast_to(b, (128, b.shape[1])) * scale).T


def fetch(sources, targets, sems):
    copies = [
        pltpu.make_async_copy(source, target, sems.at[i])
        for i, (source, target) in enumerate(zip(sources, targets))
    ]
    for copy in copies:
        copy.start()
    return copies


def pack_kernel(
    patches,
    place,
    fields_hbm,
    senders_hbm,
    near_hbm,
    x_ref,
    up_ref,
    down_ref,
    k_ref,
    n_ref,
    fields_ref,
    senders_ref,
    near_ref,
    sems,
):
    copies = fetch(
        (fields_hbm, senders_hbm, near_hbm), (fields_ref, senders_ref, near_ref), sems
    )
    for copy in copies:
        copy.wait()
    channels, members, rows = fields_ref.shape
    nodes = senders_ref.shape[1]
    nbrs = near_ref.shape[0]
    stride = rows // nodes
    halo = up_ref.shape[1]
    kx = channels * members
    x = fields_ref[...].reshape(kx, rows)
    x_ref[:kx, :] = x
    x_ref[kx:, :] = jnp.zeros((x_ref.shape[0] - kx, rows), BF16)
    senders = senders_ref[...]
    node = iota(senders.shape, 1)
    k = wrap(senders - place[0] * rows - node * stride + GRIM, rows * patches) - GRIM
    k = jnp.where(senders >= 0, k, EMPTY)
    k = pltpu.roll(k, MHALO, 1)
    k_ref[...] = k
    near = near_ref[...]
    near = wrap(near - place[0] * nodes - iota(near.shape, 1) + REACH, nodes * patches) - REACH
    n_ref[:nbrs, :] = near
    n_ref[nbrs:, :] = jnp.zeros((8 - nbrs, nodes), jnp.int32)
    near = pltpu.roll(n_ref[...], MHALO, 1)
    n_ref[...] = near
    zero = jnp.zeros((8, halo - 3 * 128), F32)
    k = k.astype(F32)[:, :128]
    extra = [k[:8], k[8:], near.astype(F32)[:, :128], zero]
    extra = jnp.concatenate(extra, axis=1).astype(BF16)
    up_ref[...] = jnp.concatenate([x[:, rows - halo :], extra], axis=0)
    down_ref[...] = jnp.concatenate([x[:, :halo], extra], axis=0)


def own_kernel(members, x_ref, k_ref, *refs):
    sources = refs[:13]
    gp_ref, edge_ref, part_ref, embed_t, mesh_t, out_t, encode_t, cols_ref = refs[13:21]
    wcat, bdec = refs[21:23]
    targets, sems = refs[23:36], refs[36]
    copies = fetch(sources, targets, sems)
    for copy in copies:
        copy.wait()
    (
        w_embed,
        b_embed,
        w_encode,
        b_encode,
        gain,
        w_receive,
        w_sender,
        b_process,
        w_update,
        w_decmesh,
        w_decgrid,
        b_decode,
        w_output,
    ) = targets
    channels, hidden = w_embed.shape
    rows = x_ref.shape[1]
    nodes = k_ref.shape[1]
    kx = channels * members
    for m in range(members):
        sp = spread(channels, members, m)
        we = dot(sp, w_embed[...]) * 0.5
        we = jnp.concatenate([we, jnp.zeros((x_ref.shape[0] - kx, hidden), F32)], axis=0)
        embed_t[m * hidden : (m + 1) * hidden, :] = we.T.astype(BF16)
        out_t[:, m * hidden : (m + 1) * hidden] = dot(sp, w_output[...]).astype(BF16)
    enc = turned(w_encode[...], 0.5)
    encode_t[...] = enc
    wcat[:hidden, :] = enc
    wcat[hidden:, :] = turned(w_decgrid[...], 0.5)
    mesh_t[0] = turned(w_sender[...], 0.5)
    mesh_t[1] = turned(w_receive[...], 0.5)
    mesh_t[2] = turned(w_update[...], 1.0)
    mesh_t[3] = turned(w_decmesh[...], 0.5)
    cols_ref[0] = column(b_embed[...], 0.5)
    cols_ref[1] = column(b_encode[...], 0.5)
    cols_ref[2] = column(b_process[...], 0.5)
    cols_ref[3] = column(gain[...], 1.0)
    bdec[...] = column(b_decode[...], 0.5)
    part_ref[...] = jnp.zeros_like(part_ref)
    block = 512
    steps = rows // block

    def step(i, carry):
        o = pl.multiple_of(i * block, block)
        lanes = pl.ds(o, block)
        pre = dot(embed_t[...], x_ref[:, lanes])
        h = silu((pre + wide(twice(cols_ref[0]), block)).astype(BF16))
        msgs = []
        for m in range(members):
            y = dot(wcat[...], h[m * hidden : (m + 1) * hidden, :])
            msgs.append(silu((y[:hidden] + wide(cols_ref[1], block)).astype(BF16)))
            gp_ref[m * hidden : (m + 1) * hidden, lanes] = (
                y[hidden:] + wide(bdec[...], block)
            ).astype(BF16)
        msg = jnp.concatenate(msgs, axis=0)

        @pl.when(i == 0)
        def _():
            edge_ref[:, :GRIM] = msg[:, :GRIM]

        @pl.when(i == steps - 1)
        def _():
            edge_ref[:, GRIM:] = msg[:, block - GRIM :]

        node = (iota(k_ref.shape, 1) + (nodes - MHALO)) % nodes
        idx = k_ref[...] + node * (rows // nodes)
        part_ref[...] += dot(msg, counts(idx, block, o))
        return carry

    lax.fori_loop(0, steps, step, 0)


def rest_kernel(
    members,
    patches,
    place,
    lo_ref,
    hi_ref,
    x_ref,
    k_ref,
    near_ref,
    sent_ref,
    gp_ref,
    edge_ref,
    part_ref,
    embed_t,
    mesh_t,
    out_t,
    encode_t,
    cols_ref,
    bout_ref,
    pred_ref,
    total_ref,
    xh_ref,
    msg_ref,
    sr_ref,
    sent_s,
    p_ref,
):
    hidden = encode_t.shape[0]
    kx = out_t.shape[0]
    channels = kx // members
    rows = x_ref.shape[1]
    halo = lo_ref.shape[1]
    both = members * hidden
    nodes = k_ref.shape[1]
    top = lo_ref.shape[0]
    xh_ref[:top, :halo] = lo_ref[...]
    xh_ref[:top, halo:] = hi_ref[...]
    xh_ref[top:, :] = jnp.zeros((xh_ref.shape[0] - top, 2 * halo), BF16)
    block = 256

    def halo_step(i, carry):
        lanes = pl.ds(pl.multiple_of(i * block, block), block)
        pre = dot(embed_t[...], xh_ref[:, lanes])
        h = silu((pre + wide(twice(cols_ref[0]), block)).astype(BF16))
        for m in range(members):
            y = dot(encode_t[...], h[m * hidden : (m + 1) * hidden, :])
            msg_ref[m * hidden : (m + 1) * hidden, lanes] = silu(
                (y + wide(cols_ref[1], block)).astype(BF16)
            )
        return carry

    lax.fori_loop(0, 2 * halo // block, halo_step, 0)
    tail = kx // 16 * 16
    lo_x = lo_ref[tail : tail + 16, :].astype(F32)[kx - tail :].astype(jnp.int32)
    hi_x = hi_ref[tail : tail + 16, :].astype(F32)[kx - tail :].astype(jnp.int32)
    slots = jnp.concatenate([lo_x[:, :128], lo_x[:, 128:256]], axis=0)
    lane = iota(slots.shape, 1)
    seam = k_ref[:, :128]
    near_by = lane * 8 + (halo - 8 * MHALO)
    own = near_by + seam
    left = jnp.where(lane < MHALO, near_by + slots, jnp.where(own < halo, own, EMPTY))
    slots = jnp.concatenate([hi_x[:, :128], hi_x[:, 128:256]], axis=0)
    near_by = lane * 8 - (rows - GRIM - 8 * (nodes - MHALO))
    own = near_by + seam
    right = jnp.where(lane >= MHALO, near_by + slots, jnp.where(own >= GRIM, own, EMPTY))
    lsum = dot(msg_ref[:, :halo], counts(left, halo, 0)) + dot(
        edge_ref[:, :GRIM], counts(left, GRIM, halo)
    )
    rsum = dot(edge_ref[:, GRIM:], counts(right, GRIM, 0)) + dot(
        msg_ref[:, halo:], counts(right, halo, GRIM)
    )
    seam = part_ref[:, :128]
    lane = iota(seam.shape, 1)
    lsum = lsum + jnp.where(lane >= MHALO, seam, 0.0)
    rsum = rsum + jnp.where(lane < MHALO, seam, 0.0)
    sums = jnp.concatenate([lsum, part_ref[:, 128:], rsum], axis=1)
    ext = sums.shape[1]
    latents = []
    for m in range(members):
        s = sums[m * hidden : (m + 1) * hidden]
        scale = lax.rsqrt(jnp.sum(s * s, axis=0, keepdims=True) * (1.0 / hidden) + 1e-5)
        latents.append((wide(cols_ref[3], ext) * s * scale).astype(BF16))
    latent = jnp.concatenate(latents, axis=1)
    send = dot(mesh_t[0], latent).astype(BF16)
    recv = (dot(mesh_t[1], latent) + wide(cols_ref[2], members * ext)).astype(BF16)
    for m in range(members):
        sr_ref[m * hidden : (m + 1) * hidden, :] = send[:, m * ext : (m + 1) * ext]
    seam = near_ref[:, :128]
    lane = iota(seam.shape, 1)
    blocks = (
        (jnp.where(lane < MHALO, lo_x[:, 256:384], seam), 0, 256),
        (near_ref[:, 128:], 0, 384),
        (jnp.where(lane >= MHALO, hi_x[:, 256:384], seam), 128, 256),
    )
    sums = []
    for b, (k, first, height) in enumerate(blocks):
        at = k + lane + (128 * b - first)
        base = jnp.concatenate(
            [recv[:, m * ext + 128 * b : m * ext + 128 * (b + 1)] for m in range(members)], axis=0
        )
        total = None
        for j in range(0, 6, 2):
            pair = jnp.concatenate([at[j : j + 1], at[j + 1 : j + 2]], axis=1)
            hot = [marks(small(pair - f), min(256, height - f)) for f in range(0, height, 256)]
            hot = hot[0] if len(hot) == 1 else jnp.concatenate(hot, axis=0)
            got = dot(sr_ref[:, first : first + height], hot).astype(BF16) + wide(base, 256)
            act = silu(got).astype(F32)
            act = act[:, :128] + act[:, 128:]
            total = act if total is None else total + act
        sums.append(total.astype(BF16))
    process = jnp.concatenate(
        [s[m * hidden : (m + 1) * hidden] for m in range(members) for s in sums], axis=1
    )
    new = (latent.astype(F32) + dot(mesh_t[2], process)).astype(BF16)
    part = dot(mesh_t[3], new).astype(BF16)
    for m in range(members):
        sr_ref[m * hidden : (m + 1) * hidden, :] = part[:, m * ext : (m + 1) * ext]
    sent = wrap(sent_ref[...] - place[0] * nodes + MHALO, nodes * patches)
    half = rows // 2
    sent_s[...] = jnp.where(iota(sent.shape, 1) >= half, sent - 128, sent).astype(F32)
    shape = (channels, x_ref.shape[0])
    fold = jnp.where(iota(shape, 1) // members == iota(shape, 0), 1.0, 0.0).astype(BF16)
    bout = (iota((kx, channels), 0) // members == iota((kx, channels), 1)).astype(F32)
    bout = jnp.sum(bout * bout_ref[...], axis=1, keepdims=True)
    bout = jnp.broadcast_to(bout, (kx, block))
    p_ref[kx:, :] = jnp.zeros((p_ref.shape[0] - kx, block), BF16)
    for b in range(2):

        def step(i, carry, b=b):
            lanes = pl.ds(pl.multiple_of(b * half + i * block, block), block)
            window = sr_ref[:, 128 * b : 128 * b + 256]
            idx = sent_s[:, lanes].astype(BF16)
            gp = gp_ref[:, lanes]
            total = None
            for j in range(idx.shape[0]):
                act = silu(dot(window, marks(idx[j : j + 1], 256)).astype(BF16) + gp)
                total = act if total is None else total + act
            delta = dot(out_t[...], total) + bout
            pred = (x_ref[:kx, lanes].astype(F32) + delta).astype(BF16)
            pred_ref[:, :, lanes] = pred.reshape(channels, members, block)
            p_ref[:kx, :] = pred
            total_ref[:, lanes] = dot(fold, p_ref[...]).astype(BF16)
            return carry

        lax.fori_loop(0, half // block, step, 0)


def week_kernel(count, total_ref, other_ref, week_ref, clim_ref, out_ref):
    ensemble = (total_ref[...].astype(F32) + other_ref[...].astype(F32)) * (1.0 / count)
    out_ref[...] = week_ref[...] + ensemble - clim_ref[...].astype(F32)


def call(kernel, outs, scratch, name, args, flops, spaces, limit=24):
    kinds = {"s": pltpu.SMEM, "v": pltpu.VMEM, "h": pltpu.HBM}
    args = [
        a if kind == "s" else pltpu.with_memory_space_constraint(a, kinds[kind])
        for a, kind in zip(args, spaces, strict=True)
    ]
    return pl.pallas_call(
        kernel,
        out_shape=outs,
        in_specs=[pl.BlockSpec(memory_space=kinds[kind]) for kind in spaces],
        out_specs=[pl.BlockSpec(memory_space=pltpu.VMEM)] * len(outs),
        scratch_shapes=scratch,
        name=name,
        compiler_params=pltpu.CompilerParams(vmem_limit_bytes=limit * 1024 * 1024),
        cost_estimate=pl.CostEstimate(flops=flops, bytes_accessed=1 << 22, transcendentals=0),
    )(*args)


def copies_of(args):
    return [pltpu.VMEM(a.shape, a.dtype) for a in args] + [pltpu.SemaphoreType.DMA((len(args),))]


def shards(
    fields,
    w_embed,
    b_embed,
    w_encode,
    b_encode,
    mesh_gain,
    w_receive,
    w_sender,
    b_process,
    w_update,
    w_decmesh,
    w_decgrid,
    b_decode,
    w_output,
    b_output,
    g2m_senders,
    m2g_senders,
    mesh_neighbours,
    climatology,
    week_sum,
):
    members, rows, channels = fields.shape
    hidden = w_encode.shape[0]
    nodes, nbrs = mesh_neighbours.shape
    slots = g2m_senders.shape[1]
    patches = lax.axis_size("patch")
    place = lax.axis_index("patch").astype(jnp.int32).reshape(1)
    kx = members * channels
    kpad = -(-kx // 256) * 256
    halo = MHALO * (rows // nodes) + GRIM
    ext = nodes + 2 * MHALO
    shape = jax.ShapeDtypeStruct
    inside = pltpu.VMEM

    args = (jnp.transpose(fields, (2, 0, 1)), g2m_senders.T, mesh_neighbours.T)
    x, from_low, from_high, k, near = call(
        functools.partial(pack_kernel, patches),
        [
            inside((kpad, rows), BF16),
            shape((kx + 8, halo), BF16),
            shape((kx + 8, halo), BF16),
            inside((slots, nodes), jnp.int32),
            inside((8, nodes), jnp.int32),
        ],
        copies_of(args),
        "pack_halo",
        (place,) + args,
        10**7,
        "shhh",
    )
    up = [(i, (i + 1) % patches) for i in range(patches)]
    down = [(target, source) for source, target in up]
    lo = lax.ppermute(from_low, "patch", up)
    hi = lax.ppermute(from_high, "patch", down)

    args = (
        w_embed,
        b_embed[None],
        w_encode,
        b_encode[None],
        mesh_gain[None],
        w_receive,
        w_sender,
        b_process[None],
        w_update,
        w_decmesh,
        w_decgrid,
        b_decode[None],
        w_output.T,
    )
    own = call(
        functools.partial(own_kernel, members),
        [
            inside((members * hidden, rows), BF16),
            inside((members * hidden, 2 * GRIM), BF16),
            inside((members * hidden, nodes), F32),
            inside((members * hidden, kpad), BF16),
            inside((4, hidden, hidden), BF16),
            inside((kx, members * hidden), BF16),
            inside((hidden, hidden), BF16),
            inside((4, hidden, 128), F32),
        ],
        [pltpu.VMEM((2 * hidden, hidden), BF16), pltpu.VMEM((hidden, 128), F32)]
        + copies_of(args),
        "own_rows",
        (x, k) + args,
        10**10,
        "vv" + "h" * len(args),
    )
    pred, total = call(
        functools.partial(rest_kernel, members, patches),
        [shape((channels, members, rows), BF16), shape((channels, rows), BF16)],
        [
            pltpu.VMEM((kpad, 2 * halo), BF16),
            pltpu.VMEM((members * hidden, 2 * halo), BF16),
            pltpu.VMEM((members * hidden, ext), BF16),
            pltpu.VMEM((m2g_senders.shape[1], rows), F32),
            pltpu.VMEM((kpad, 256), BF16),
        ],
        "halo_mesh_decode",
        (place, lo, hi, x, k, near, m2g_senders.T) + tuple(own) + (b_output[None],),
        2 * 10**10,
        "s" + "v" * 15,
    )
    prediction = jnp.transpose(pred, (1, 2, 0))
    other = lax.ppermute(total, "member", [(0, 1), (1, 0)])
    (week_total,) = call(
        functools.partial(week_kernel, members * lax.axis_size("member")),
        [shape((channels, rows), F32)],
        [],
        "week",
        (total, other, week_sum.T, climatology.T),
        10**6,
        "vvvv",
    )
    return (prediction, week_total.T)


def solution(mesh):
    grid = P(("groups", "member"), "patch", None)
    node = P("patch", None)
    week = P(("groups", "patch"), None)
    return jax.shard_map(
        shards,
        mesh=mesh,
        in_specs=(grid,) + (P(),) * 14 + (node,) * 4 + (week,),
        out_specs=(grid, week),
        check_vma=False,
    )
```

time: 297 us -> 43.5 us (0.15)
  local copies, waits for them, and re-layouts: 153 us -> 0.02 us
  other arithmetic: 64 us -> 0 us
  Pallas kernels: 0 us -> 34.8 us
  waiting for transfers between devices: 26.1 us -> 1.68 us
  matrix products: 23.3 us -> 0 us
  between operations: 14.5 us -> 0.7 us
  starting transfers between devices: 16 us -> 6.1 us
    gather x10 -> x0, local copies, waits for them, and re-layouts: 129 us -> none  [the longest x3 68.3 us: shards(): jnp.take(mesh_part, dec_local[:, column], axis=1) + grid_part]
    pallas_call x0 -> x4, Pallas kernels: none -> 34.8 us  [call(): pl.pallas_call(kernel, out_shape=outs, in_specs=[pl.BlockSpec(memory_spac...]
    convert_element_type x3 -> x0, other arithmetic: 23.4 us -> none  [the longest x1 19.2 us: rounded(): values.astype(jnp.bfloat16)]
    dot_general x7 -> x0, matrix products: 23.3 us -> none  [the longest x1 7.81 us: shards(): jnp.dot(grid_latent.reshape(members * grid_rows, hidden), w_decgrid, pref...]
    reduce_sum x3 -> x0, other arithmetic: 20.4 us -> none  [the longest x1 17.4 us: shards(): mesh_sum = jnp.sum(gathered.astype(jnp.float32), axis=2)]
    psum x1 -> x0, waiting for transfers between devices: 20.3 us -> none  [shards(): lax.psum(local_total.astype(jnp.bfloat16), 'member').astype(jnp.float32)]
    concatenate x1 -> x0, other arithmetic: 17.8 us -> none  [extended_2(): block = jnp.concatenate([low, block, high], axis=dim)]
    reshape x3 -> x0, local copies, waits for them, and re-layouts: 16.9 us -> none  [the longest x1 16.4 us: shards(): messages = message.astype(jnp.bfloat16).reshape(members, -1, hidden)]
  transfers between devices with their start and end apart: 7 -> 3, of which waited for: 4 -> 1; matrix products, arithmetic and copies ran while one was open for 3% -> 0% of each run, Pallas kernels for 0% -> 34%
where the time goes in v1:
time: 43.5 us; the launch traced here: 43.3 us
  Pallas kernels  34.8 us (80%)
  starting transfers between devices  6.1 us (14%)
  waiting for transfers between devices  1.68 us (4%)
  between operations  0.7 us (2%)
    pallas_call x4, Pallas kernels, call(): pl.pallas_call(kernel, out_shape=outs, in_specs=[pl.BlockSpec(memory_spac...  34.8 us
    ppermute x1, starting transfers between devices, shards(): hi = lax.ppermute(from_high, 'patch', down)  3.1 us
    ppermute x1, starting transfers between devices, shards(): lo = lax.ppermute(from_low, 'patch', up)  2.99 us
    ppermute x1, waiting for transfers between devices, shards(): other = lax.ppermute(total, 'member', [(0, 1), (1, 0)])  1.67 us
  transfers between devices with their start and end apart: 3, of which 1 were waited for; matrix products, arithmetic and copies ran while one was open for 0% of the time, Pallas kernels for 34%

profile of v1, /device:TPU:0, one launch (start us, length us, event | category | flops | bytes accessed | tf_op | source)
XLA Modules:
  0.0 43.3 jit_solution(1494470305438237874)
XLA Ops:
  0.6 1.3 %pack_halo.1 = (bf16[256,2048]{1,0:T(8,128)(2,1)S(1)}, bf16[176,640]{1,0:T(8,128)(2,1)S(1)}, bf16[176,640]{1,0:T(8,128)(2,1)S(1)}, s32[16,256]{1,0:T(8,128)S(1)}, s32[8,256]{1,0:T(8,128)S(1)}) custom-call(s32[1]{0:T(128)} %bitcast.place, bf16[84,2,2048]{2,1,0:T(2,128)(2,1)} %bitcast.21, s32[16,256]{1,0:T(8,128)} %bitcast.22, s32[6,256]{1,0:T(8,128)} %bitcast.23), custom_call_target="tpu_custom_call" | custom-call | flops 10000000 | bytes 4194304 | tf_op jit(solution)/shard_map/pack_halo/pallas_call | solution.py:379
  2.0 3.0 %collective-permute-start = (bf16[176,640]{1,0:T(8,128)(2,1)S(1)}, bf16[176,640]{1,0:T(8,128)(2,1)S(1)}, u32[]{:S(2)}, u32[]{:S(2)}) collective-permute-start(bf16[176,640]{1,0:T(8,128)(2,1)S(1)} %get-tuple-element.17), channel_id=1, source_target_pairs={{0,2},{2,4},{4,6},{6,8},{8,10},{10,12},{12,14},{14,0},{1,3},{3,5},... | collective-permute-start | bytes 675848 | tf_op jit(solution)/shard_map/ppermute | solution.py:448
  5.0 3.1 %collective-permute-start.1 = (bf16[176,640]{1,0:T(8,128)(2,1)S(1)}, bf16[176,640]{1,0:T(8,128)(2,1)S(1)}, u32[]{:S(2)}, u32[]{:S(2)}) collective-permute-start(bf16[176,640]{1,0:T(8,128)(2,1)S(1)} %get-tuple-element.18), channel_id=1, source_target_pairs={{2,0},{4,2},{6,4},{8,6},{10,8},{12,10},{14,12},{0,14},{3,1},{5,3},... | collective-permute-start | bytes 675848 | tf_op jit(solution)/shard_map/ppermute | solution.py:449
  8.1 0.0 copy-start.2
  8.1 0.0 copy-start.3
  8.1 14.7 %own_rows.1 = (bf16[1024,2048]{1,0:T(8,128)(2,1)S(1)}, bf16[1024,256]{1,0:T(8,128)(2,1)S(1)}, f32[1024,256]{1,0:T(8,128)S(1)}, bf16[1024,256]{1,0:T(8,128)(2,1)S...) custom-call(bf16[256,2048]{1,0:T(8,128)(2,1)S(1)} %get-tuple-element, ...), custom_call_target="tpu_custom_call" | custom-call | flops 10000000000 | bytes 4194304 | tf_op jit(solution)/shard_map/own_rows/pallas_call | solution.py:379
  22.8 0.0 collective-permute-done.lo_ref
  22.8 0.0 collective-permute-done.1.hi_ref
  22.8 0.0 copy-done.2
  22.8 0.0 copy-done.3
  22.9 0.0 copy-start
  22.9 0.0 copy-start.1
  22.9 17.7 %halo_mesh_decode.1 = (bf16[84,2,2048]{2,1,0:T(2,128)(2,1)}, bf16[84,2048]{1,0:T(8,128)(2,1)S(1)}) custom-call(s32[1]{0:T(128)} %bitcast.place, bf16[176,640]{1,0:T(8,128)(2,1)S(1)} %collective-permute-done.lo_ref, bf16[176,640]{1,0:T(8,128)(2,1)S(1)} %collective-permute-done.1.hi_ref, bf16[256,2048]{1,0:T(8,128)(2,1)S(1)} %get-tuple-element.19.x_ref, ...), custom_call_target="tpu_custom_call" | custom-call | flops 20000000000 | bytes 4194304 | tf_op jit(solution)/shard_map/halo_mesh_decode/pallas_call | solution.py:379
  40.6 0.0 collective-permute-start.2
  40.6 1.7 %collective-permute-done.2.other_ref = bf16[84,2048]{1,0:T(8,128)(2,1)S(1)} collective-permute-done((bf16[84,2048]{1,0:T(8,128)(2,1)S(1)}, bf16[84,2048]{1,0:T(8,128)(2,1)S(1)}, u32[]{:S(2)}, u32[]{:S(2)}) %collective-permute-start.2) | collective-permute-done | bytes 344096 | tf_op jit(solution)/shard_map/ppermute | solution.py:501
  42.3 0.0 copy-done
  42.3 0.0 copy-done.1
  42.3 1.0 %week.1 = f32[84,2048]{1,0:T(8,128)} custom-call(bf16[84,2048]{1,0:T(8,128)(2,1)S(1)} %get-tuple-element.31.total_ref, bf16[84,2048]{1,0:T(8,128)(2,1)S(1)} %collective-permute-done.2.other_ref, f32[84,2048]{1,0:T(8,128)S(1)} %bitcast.16, bf16[84,2048]{1,0:T(8,128)(2,1)S(1)} %bitcast.17), custom_call_target="tpu_custom_call" | custom-call | flops 1000000 | bytes 4194304 | tf_op jit(solution)/shard_map/week/pallas_call | solution.py:379
Async XLA Ops:
  2.0 20.8 %collective-permute-start = (bf16[176,640]{1,0:T(8,128)(2,1)S(1)}, bf16[176,640]{1,0:T(8,128)(2,1)S(1)}, u32[]{:S(2)}, u32[]{:S(2)}) collective-permute-start(bf16[176,640]{1,0:T(8,128)(2,1)S(1)} %get-tuple-element.17), channel_id=1, source_target_pairs={{0,2},{2,4},{4,6},{6,8},{8,10},{10,12},{12,14},{14,0},{1,3},{3,5},... | collective-permute-start | bytes 675848 | tf_op jit(solution)/shard_map/ppermute | solution.py:448
  5.0 17.9 %collective-permute-start.1 = (bf16[176,640]{1,0:T(8,128)(2,1)S(1)}, bf16[176,640]{1,0:T(8,128)(2,1)S(1)}, u32[]{:S(2)}, u32[]{:S(2)}) collective-permute-start(bf16[176,640]{1,0:T(8,128)(2,1)S(1)} %get-tuple-element.18), channel_id=1, source_target_pairs={{2,0},{4,2},{6,4},{8,6},{10,8},{12,10},{14,12},{0,14},{3,1},{5,3},... | collective-permute-start | bytes 675848 | tf_op jit(solution)/shard_map/ppermute | solution.py:449
  8.1 14.8 %copy-start.2 = (s32[2048,3]{0,1:T(4,128)S(1)}, s32[2048,3]{0,1:T(4,128)}, u32[]{:S(2)}) copy-start(s32[2048,3]{0,1:T(4,128)} %param.36) | copy-start | bytes 73732
  8.1 14.8 %copy-start.3 = (f32[84]{0:T(128)S(1)}, f32[84]{0:T(128)}, u32[]{:S(2)}) copy-start(f32[84]{0:T(128)} %param.34) | copy-start | bytes 1012
  22.9 19.4 %copy-start = (f32[2048,84]{0,1:T(8,128)S(1)}, f32[2048,84]{0,1:T(8,128)}, u32[]{:S(2)}) copy-start(f32[2048,84]{0,1:T(8,128)} %param.39) | copy-start | bytes 2064388
  22.9 19.4 %copy-start.1 = (bf16[2048,84]{0,1:T(8,128)(2,1)S(1)}, bf16[2048,84]{0,1:T(8,128)(2,1)}, u32[]{:S(2)}) copy-start(bf16[2048,84]{0,1:T(8,128)(2,1)} %param.38) | copy-start | bytes 1032196
  40.6 1.7 %collective-permute-start.2 = (bf16[84,2048]{1,0:T(8,128)(2,1)S(1)}, bf16[84,2048]{1,0:T(8,128)(2,1)S(1)}, u32[]{:S(2)}, u32[]{:S(2)}) collective-permute-start(bf16[84,2048]{1,0:T(8,128)(2,1)S(1)} %get-tuple-element.31.total_ref), channel_id=1, source_target_pairs={{0,1},{1,0},{2,3},{3,2},{4,5},{5,4},{6,7},{7,6},{8,9},{9,8},{10,11... | collective-permute-start | bytes 1032200 | tf_op jit(solution)/shard_map/ppermute | solution.py:501

commit v2 on v1

--- a/solution.py
+++ b/solution.py
@@ -138,29 +138,37 @@
     down_ref[...] = jnp.concatenate([x[:, :halo], extra], axis=0)
 
 
-def own_kernel(members, x_ref, k_ref, *refs):
-    sources = refs[:13]
-    gp_ref, edge_ref, part_ref, embed_t, mesh_t, out_t, encode_t, cols_ref = refs[13:21]
-    wcat, bdec = refs[21:23]
-    targets, sems = refs[23:36], refs[36]
-    copies = fetch(sources, targets, sems)
-    for copy in copies:
-        copy.wait()
-    (
-        w_embed,
-        b_embed,
-        w_encode,
-        b_encode,
-        gain,
-        w_receive,
-        w_sender,
-        b_process,
-        w_update,
-        w_decmesh,
-        w_decgrid,
-        b_decode,
-        w_output,
-    ) = targets
+def own_kernel(
+    members,
+    x_ref,
+    k_ref,
+    w_embed,
+    b_embed,
+    w_encode,
+    b_encode,
+    gain,
+    w_receive,
+    w_sender,
+    b_process,
+    w_update,
+    w_decmesh,
+    w_decgrid,
+    b_decode,
+    w_output,
+    gp_ref,
+    edge_ref,
+    part_ref,
+    embed_t,
+    mesh_t,
+    out_t,
+    encode_t,
+    cols_ref,
+    wcat,
+    bdec,
+    h_ref,
+    msg_ref,
+    count_ref,
+):
     channels, hidden = w_embed.shape
     rows = x_ref.shape[1]
     nodes = k_ref.shape[1]
@@ -184,38 +192,33 @@
     cols_ref[2] = column(b_process[...], 0.5)
     cols_ref[3] = column(gain[...], 1.0)
     bdec[...] = column(b_decode[...], 0.5)
-    part_ref[...] = jnp.zeros_like(part_ref)
-    block = 512
-    steps = rows // block
-
-    def step(i, carry):
-        o = pl.multiple_of(i * block, block)
-        lanes = pl.ds(o, block)
-        pre = dot(embed_t[...], x_ref[:, lanes])
-        h = silu((pre + wide(twice(cols_ref[0]), block)).astype(BF16))
-        msgs = []
-        for m in range(members):
-            y = dot(wcat[...], h[m * hidden : (m + 1) * hidden, :])
-            msgs.append(silu((y[:hidden] + wide(cols_ref[1], block)).astype(BF16)))
-            gp_ref[m * hidden : (m + 1) * hidden, lanes] = (
-                y[hidden:] + wide(bdec[...], block)
-            ).astype(BF16)
-        msg = jnp.concatenate(msgs, axis=0)
-
-        @pl.when(i == 0)
-        def _():
-            edge_ref[:, :GRIM] = msg[:, :GRIM]
-
-        @pl.when(i == steps - 1)
-        def _():
-            edge_ref[:, GRIM:] = msg[:, block - GRIM :]
-
-        node = (iota(k_ref.shape, 1) + (nodes - MHALO)) % nodes
-        idx = k_ref[...] + node * (rows // nodes)
-        part_ref[...] += dot(msg, counts(idx, block, o))
-        return carry
-
-    lax.fori_loop(0, steps, step, 0)
+    pre = dot(embed_t[...], x_ref[...])
+    h_ref[...] = silu((pre + wide(twice(cols_ref[0]), rows)).astype(BF16))
+    for m in range(members):
+        part = slice(m * hidden, (m + 1) * hidden)
+        y = dot(wcat[...], h_ref[part, :])
+        msg_ref[part, :] = silu((y[:hidden] + wide(cols_ref[1], rows)).astype(BF16))
+        gp_ref[part, :] = (y[hidden:] + wide(bdec[...], rows)).astype(BF16)
+    edge_ref[:, :GRIM] = msg_ref[:, :GRIM]
+    edge_ref[:, GRIM:] = msg_ref[:, rows - GRIM :]
+    stride = rows // nodes
+    node = (iota(k_ref.shape, 1) + (nodes - MHALO)) % nodes
+    idx = k_ref[...] + node * stride
+    for base in range(0, rows, 128):
+        near = small(idx - base)
+        first = max(0, (base - GRIM - stride) // stride)
+        last = min(nodes - 1, (base + 127 + GRIM) // stride)
+        touched = {(r + MHALO) % nodes // 128 for r in range(first, last + 1)}
+        for tile in range(nodes // 128):
+            lanes = slice(128 * tile, 128 * (tile + 1))
+            if tile in touched:
+                total = marks(near[0:1, lanes], 128)
+                for slot in range(1, idx.shape[0]):
+                    total = total + marks(near[slot : slot + 1, lanes], 128)
+            else:
+                total = jnp.zeros((128, 128), BF16)
+            count_ref[base : base + 128, lanes] = total
+    part_ref[...] = dot(msg_ref[...], count_ref[...])
 
 
 def rest_kernel(
@@ -242,7 +245,7 @@
     xh_ref,
     msg_ref,
     sr_ref,
-    sent_s,
+    sum_ref,
     p_ref,
 ):
     hidden = encode_t.shape[0]
@@ -256,20 +259,11 @@
     xh_ref[:top, :halo] = lo_ref[...]
     xh_ref[:top, halo:] = hi_ref[...]
     xh_ref[top:, :] = jnp.zeros((xh_ref.shape[0] - top, 2 * halo), BF16)
-    block = 256
-
-    def halo_step(i, carry):
-        lanes = pl.ds(pl.multiple_of(i * block, block), block)
-        pre = dot(embed_t[...], xh_ref[:, lanes])
-        h = silu((pre + wide(twice(cols_ref[0]), block)).astype(BF16))
-        for m in range(members):
-            y = dot(encode_t[...], h[m * hidden : (m + 1) * hidden, :])
-            msg_ref[m * hidden : (m + 1) * hidden, lanes] = silu(
-                (y + wide(cols_ref[1], block)).astype(BF16)
-            )
-        return carry
-
-    lax.fori_loop(0, 2 * halo // block, halo_step, 0)
+    h = silu((dot(embed_t[...], xh_ref[...]) + wide(twice(cols_ref[0]), 2 * halo)).astype(BF16))
+    for m in range(members):
+        part = slice(m * hidden, (m + 1) * hidden)
+        y = dot(encode_t[...], h[part])
+        msg_ref[part, :] = silu((y + wide(cols_ref[1], 2 * halo)).astype(BF16))
     tail = kx // 16 * 16
     lo_x = lo_ref[tail : tail + 16, :].astype(F32)[kx - tail :].astype(jnp.int32)
     hi_x = hi_ref[tail : tail + 16, :].astype(F32)[kx - tail :].astype(jnp.int32)
@@ -337,32 +331,26 @@
         sr_ref[m * hidden : (m + 1) * hidden, :] = part[:, m * ext : (m + 1) * ext]
     sent = wrap(sent_ref[...] - place[0] * nodes + MHALO, nodes * patches)
     half = rows // 2
-    sent_s[...] = jnp.where(iota(sent.shape, 1) >= half, sent - 128, sent).astype(F32)
+    idx = small(jnp.where(iota(sent.shape, 1) >= half, sent - 128, sent))
+    for b in range(2):
+        lanes = slice(b * half, (b + 1) * half)
+        window = sr_ref[:, 128 * b : 128 * b + 256]
+        total = None
+        for j in range(idx.shape[0]):
+            got = dot(window, marks(idx[j : j + 1, lanes], 256)).astype(BF16)
+            act = silu(got + gp_ref[:, lanes])
+            total = act if total is None else total + act
+        sum_ref[:, lanes] = total
+    bout = (iota((kx, channels), 0) // members == iota((kx, channels), 1)).astype(F32)
+    bout = jnp.sum(bout * bout_ref[...], axis=1, keepdims=True)
+    delta = dot(out_t[...], sum_ref[...]) + bout
+    pred = (x_ref[:kx, :].astype(F32) + delta).astype(BF16)
+    pred_ref[...] = pred.reshape(channels, members, rows)
+    p_ref[:kx, :] = pred
+    p_ref[kx:, :] = jnp.zeros((p_ref.shape[0] - kx, rows), BF16)
     shape = (channels, x_ref.shape[0])
     fold = jnp.where(iota(shape, 1) // members == iota(shape, 0), 1.0, 0.0).astype(BF16)
-    bout = (iota((kx, channels), 0) // members == iota((kx, channels), 1)).astype(F32)
-    bout = jnp.sum(bout * bout_ref[...], axis=1, keepdims=True)
-    bout = jnp.broadcast_to(bout, (kx, block))
-    p_ref[kx:, :] = jnp.zeros((p_ref.shape[0] - kx, block), BF16)
-    for b in range(2):
-
-        def step(i, carry, b=b):
-            lanes = pl.ds(pl.multiple_of(b * half + i * block, block), block)
-            window = sr_ref[:, 128 * b : 128 * b + 256]
-            idx = sent_s[:, lanes].astype(BF16)
-            gp = gp_ref[:, lanes]
-            total = None
-            for j in range(idx.shape[0]):
-                act = silu(dot(window, marks(idx[j : j + 1], 256)).astype(BF16) + gp)
-                total = act if total is None else total + act
-            delta = dot(out_t[...], total) + bout
-            pred = (x_ref[:kx, lanes].astype(F32) + delta).astype(BF16)
-            pred_ref[:, :, lanes] = pred.reshape(channels, members, block)
-            p_ref[:kx, :] = pred
-            total_ref[:, lanes] = dot(fold, p_ref[...]).astype(BF16)
-            return carry
-
-        lax.fori_loop(0, half // block, step, 0)
+    total_ref[...] = dot(fold, p_ref[...]).astype(BF16)
 
 
 def week_kernel(count, total_ref, other_ref, week_ref, clim_ref, out_ref):
@@ -371,9 +359,9 @@
 
 
 def call(kernel, outs, scratch, name, args, flops, spaces, limit=24):
-    kinds = {"s": pltpu.SMEM, "v": pltpu.VMEM, "h": pltpu.HBM}
+    kinds = {"s": pltpu.SMEM, "v": pltpu.VMEM, "h": pltpu.HBM, "f": pltpu.VMEM}
     args = [
-        a if kind == "s" else pltpu.with_memory_space_constraint(a, kinds[kind])
+        a if kind in "sf" else pltpu.with_memory_space_constraint(a, kinds[kind])
         for a, kind in zip(args, spaces, strict=True)
     ]
     return pl.pallas_call(
@@ -432,15 +420,15 @@
         functools.partial(pack_kernel, patches),
         [
             inside((kpad, rows), BF16),
-            shape((kx + 8, halo), BF16),
-            shape((kx + 8, halo), BF16),
+            inside((kx + 8, halo), BF16),
+            inside((kx + 8, halo), BF16),
             inside((slots, nodes), jnp.int32),
             inside((8, nodes), jnp.int32),
         ],
         copies_of(args),
         "pack_halo",
         (place,) + args,
-        10**7,
+        2 * 10**10,
         "shhh",
     )
     up = [(i, (i + 1) % patches) for i in range(patches)]
@@ -475,27 +463,34 @@
             inside((hidden, hidden), BF16),
             inside((4, hidden, 128), F32),
         ],
-        [pltpu.VMEM((2 * hidden, hidden), BF16), pltpu.VMEM((hidden, 128), F32)]
-        + copies_of(args),
+        [
+            pltpu.VMEM((2 * hidden, hidden), BF16),
+            pltpu.VMEM((hidden, 128), F32),
+            pltpu.VMEM((members * hidden, rows), BF16),
+            pltpu.VMEM((members * hidden, rows), BF16),
+            pltpu.VMEM((rows, nodes), BF16),
+        ],
         "own_rows",
         (x, k) + args,
         10**10,
-        "vv" + "h" * len(args),
+        "vv" + "f" * len(args),
+        32,
     )
     pred, total = call(
         functools.partial(rest_kernel, members, patches),
-        [shape((channels, members, rows), BF16), shape((channels, rows), BF16)],
+        [inside((channels, members, rows), BF16), inside((channels, rows), BF16)],
         [
             pltpu.VMEM((kpad, 2 * halo), BF16),
             pltpu.VMEM((members * hidden, 2 * halo), BF16),
             pltpu.VMEM((members * hidden, ext), BF16),
-            pltpu.VMEM((m2g_senders.shape[1], rows), F32),
-            pltpu.VMEM((kpad, 256), BF16),
+            pltpu.VMEM((members * hidden, rows), BF16),
+            pltpu.VMEM((kpad, rows), BF16),
         ],
         "halo_mesh_decode",
         (place, lo, hi, x, k, near, m2g_senders.T) + tuple(own) + (b_output[None],),
         2 * 10**10,
         "s" + "v" * 15,
+        32,
     )
     prediction = jnp.transpose(pred, (1, 2, 0))
     other = lax.ppermute(total, "member", [(0, 1), (1, 0)])

time: 43.5 us -> 34 us (0.78)
  Pallas kernels: 34.8 us -> 25 us
  local copies, waits for them, and re-layouts: 0.02 us -> 0.93 us
  waiting for transfers between devices: 1.68 us -> 0.82 us
    pallas_call x4, Pallas kernels: 34.8 us -> 25 us  [call(): pl.pallas_call(kernel, out_shape=outs, in_specs=[pl.BlockSpec(memory_spac...]
    unnamed x8 -> x35, local copies, waits for them, and re-layouts: 0.02 us -> 0.93 us
    ppermute x1, waiting for transfers between devices: 1.67 us -> 0.81 us  [shards(): other = lax.ppermute(total, 'member', [(0, 1), (1, 0)])]
  transfers between devices with their start and end apart: 3 -> 3, of which waited for: 1 -> 1; matrix products, arithmetic and copies ran while one was open for 0% -> 3% of each run, Pallas kernels for 34% -> 26%
where the time goes in v2:
time: 34 us; the launch traced here: 33.8 us
  Pallas kernels  25 us (74%)
  starting transfers between devices  6.17 us (18%)
  local copies, waits for them, and re-layouts  0.93 us (3%)
  between operations  0.91 us (3%)
  waiting for transfers between devices  0.82 us (2%)
    pallas_call x4, Pallas kernels, call(): pl.pallas_call(kernel, out_shape=outs, in_specs=[pl.BlockSpec(memory_spac...  25 us
    ppermute x1, starting transfers between devices, shards(): hi = lax.ppermute(from_high, 'patch', down)  3.1 us
    ppermute x1, starting transfers between devices, shards(): lo = lax.ppermute(from_low, 'patch', up)  2.99 us
    unnamed x35, local copies, waits for them, and re-layouts  0.93 us
    ppermute x1, waiting for transfers between devices, shards(): other = lax.ppermute(total, 'member', [(0, 1), (1, 0)])  0.81 us
  transfers between devices with their start and end apart: 3, of which 1 were waited for; matrix products, arithmetic and copies ran while one was open for 3% of the time, Pallas kernels for 26%

profile of v2, /device:TPU:0, one launch (start us, length us, event | category | flops | bytes accessed | tf_op | source)
XLA Modules:
  0.0 33.8 jit_solution(17036048368519860851)
XLA Ops:
  0.6 0.0 copy-start.2
  0.7 0.0 copy-start.3
  0.7 0.0 copy-start.4
  0.7 0.0 copy-start.5
  0.7 0.0 copy-start.6
  0.7 0.0 copy-start.7
  0.7 0.0 copy-start.8
  0.7 0.0 copy-start.9
  0.7 0.0 copy-start.11
  0.7 0.0 copy-start.12
  0.7 0.0 copy-start.13
  0.8 0.0 copy-start.14
  0.8 0.0 copy-start.15
  0.8 1.5 %pack_halo.1 = (bf16[256,2048]{1,0:T(8,128)(2,1)S(1)}, bf16[176,640]{1,0:T(8,128)(2,1)S(1)}, bf16[176,640]{1,0:T(8,128)(2,1)S(1)}, s32[16,256]{1,0:T(8,128)S(1)}, s32[8,256]{1,0:T(8,128)S(1)}) custom-call(s32[1]{0:T(128)} %bitcast.place, bf16[84,2,2048]{2,1,0:T(2,128)(2,1)} %bitcast.28, s32[16,256]{1,0:T(8,128)} %bitcast.29, s32[6,256]{1,0:T(8,128)} %bitcast.30), custom_call_target="tpu_custom_call" | custom-call | flops 20000000000 | bytes 4194304 | tf_op jit(solution)/shard_map/pack_halo/pallas_call | solution.py:367
  2.3 3.0 %collective-permute-start = (bf16[176,640]{1,0:T(8,128)(2,1)S(1)}, bf16[176,640]{1,0:T(8,128)(2,1)S(1)}, u32[]{:S(2)}, u32[]{:S(2)}) collective-permute-start(bf16[176,640]{1,0:T(8,128)(2,1)S(1)} %get-tuple-element.17), channel_id=1, source_target_pairs={{0,2},{2,4},{4,6},{6,8},{8,10},{10,12},{12,14},{14,0},{1,3},{3,5},... | collective-permute-start | bytes 675848 | tf_op jit(solution)/shard_map/ppermute | solution.py:436
  5.3 3.1 %collective-permute-start.1 = (bf16[176,640]{1,0:T(8,128)(2,1)S(1)}, bf16[176,640]{1,0:T(8,128)(2,1)S(1)}, u32[]{:S(2)}, u32[]{:S(2)}) collective-permute-start(bf16[176,640]{1,0:T(8,128)(2,1)S(1)} %get-tuple-element.18), channel_id=1, source_target_pairs={{2,0},{4,2},{6,4},{8,6},{10,8},{12,10},{14,12},{0,14},{3,1},{5,3},... | collective-permute-start | bytes 675848 | tf_op jit(solution)/shard_map/ppermute | solution.py:437
  8.4 0.0 copy-done.2
  8.4 0.0 copy-done.3
  8.4 0.0 copy-done.4
  8.4 0.0 copy-done.5
  8.4 0.0 copy-done.6
  8.4 0.0 copy-done.7
  8.4 0.0 copy-done.8
  8.4 0.0 copy-done.9
  8.4 0.0 copy-done.11
  8.4 0.0 copy-done.12
  8.4 0.0 copy-done.13
  8.5 0.0 copy-done.14
  8.5 0.0 copy-done.15
  8.5 0.0 copy-start.10
  8.5 0.0 copy-start.16
  8.5 8.8 %own_rows.1 = (bf16[1024,2048]{1,0:T(8,128)(2,1)S(1)}, bf16[1024,256]{1,0:T(8,128)(2,1)S(1)}, f32[1024,256]{1,0:T(8,128)S(1)}, bf16[1024,256]{1,0:T(8,128)(2,1)S...) custom-call(bf16[256,2048]{1,0:T(8,128)(2,1)S(1)} %get-tuple-element, ...), custom_call_target="tpu_custom_call" | custom-call | flops 10000000000 | bytes 4194304 | tf_op jit(solution)/shard_map/own_rows/pallas_call | solution.py:367
  17.3 0.0 collective-permute-done.lo_ref
  17.3 0.0 collective-permute-done.1.hi_ref
  17.4 0.0 copy-done.10
  17.4 0.0 copy-done.16
  17.4 0.0 copy-start
  17.4 0.0 copy-start.1
  17.4 13.7 %halo_mesh_decode.1 = (bf16[84,2,2048]{2,1,0:T(2,128)(2,1)S(1)}, bf16[84,2048]{1,0:T(8,128)(2,1)S(1)}) custom-call(s32[1]{0:T(128)} %bitcast.place, bf16[176,640]{1,0:T(8,128)(2,1)S(1)} %collective-permute-done.lo_ref, bf16[176,640]{1,0:T(8,128)(2,1)S(1)} %collective-permute-done.1.hi_ref, bf16[256,2048]{1,0:T(8,128)(2,1)S(1)} %get-tuple-element.19.x_ref, ...), custom_call_target="tpu_custom_call" | custom-call | flops 20000000000 | bytes 4194304 | tf_op jit(solution)/shard_map/halo_mesh_decode/pallas_call | solution.py:367
  31.1 0.1 collective-permute-start.2
  31.1 0.8 %copy.22 = bf16[2,2048,84]{1,0,2:T(2,128)(2,1)} copy(bf16[2,2048,84]{1,0,2:T(2,128)(2,1)S(1)} %bitcast.16) | data formatting | bytes 1376256
  32.0 0.8 %collective-permute-done.2.other_ref = bf16[84,2048]{1,0:T(8,128)(2,1)S(1)} collective-permute-done((bf16[84,2048]{1,0:T(8,128)(2,1)S(1)}, bf16[84,2048]{1,0:T(8,128)(2,1)S(1)}, u32[]{:S(2)}, u32[]{:S(2)}) %collective-permute-start.2) | collective-permute-done | bytes 344096 | tf_op jit(solution)/shard_map/ppermute | solution.py:496
  32.8 0.0 copy-done
  32.8 0.0 copy-done.1
  32.8 1.0 %week.1 = f32[84,2048]{1,0:T(8,128)} custom-call(bf16[84,2048]{1,0:T(8,128)(2,1)S(1)} %get-tuple-element.31.total_ref, bf16[84,2048]{1,0:T(8,128)(2,1)S(1)} %collective-permute-done.2.other_ref, f32[84,2048]{1,0:T(8,128)S(1)} %bitcast.17, bf16[84,2048]{1,0:T(8,128)(2,1)S(1)} %bitcast.18), custom_call_target="tpu_custom_call" | custom-call | flops 1000000 | bytes 4194304 | tf_op jit(solution)/shard_map/week/pallas_call | solution.py:367
Async XLA Ops:
  0.6 7.7 %copy-start.2 = (bf16[512,512]{1,0:T(8,128)(2,1)S(1)}, bf16[512,512]{1,0:T(8,128)(2,1)}, u32[]{:S(2)}) copy-start(bf16[512,512]{1,0:T(8,128)(2,1)} %w_encode.1) | copy-start | bytes 1572868
  0.7 7.7 %copy-start.3 = (bf16[512,512]{1,0:T(8,128)(2,1)S(1)}, bf16[512,512]{1,0:T(8,128)(2,1)}, u32[]{:S(2)}) copy-start(bf16[512,512]{1,0:T(8,128)(2,1)} %w_receive.1) | copy-start | bytes 1572868
  0.7 7.7 %copy-start.4 = (bf16[512,512]{1,0:T(8,128)(2,1)S(1)}, bf16[512,512]{1,0:T(8,128)(2,1)}, u32[]{:S(2)}) copy-start(bf16[512,512]{1,0:T(8,128)(2,1)} %w_sender.1) | copy-start | bytes 1572868
  0.7 7.7 %copy-start.5 = (bf16[512,512]{1,0:T(8,128)(2,1)S(1)}, bf16[512,512]{1,0:T(8,128)(2,1)}, u32[]{:S(2)}) copy-start(bf16[512,512]{1,0:T(8,128)(2,1)} %w_update.1) | copy-start | bytes 1572868
  0.7 7.7 %copy-start.6 = (bf16[512,512]{1,0:T(8,128)(2,1)S(1)}, bf16[512,512]{1,0:T(8,128)(2,1)}, u32[]{:S(2)}) copy-start(bf16[512,512]{1,0:T(8,128)(2,1)} %w_decmesh.1) | copy-start | bytes 1572868
  0.7 7.7 %copy-start.7 = (bf16[512,512]{1,0:T(8,128)(2,1)S(1)}, bf16[512,512]{1,0:T(8,128)(2,1)}, u32[]{:S(2)}) copy-start(bf16[512,512]{1,0:T(8,128)(2,1)} %w_decgrid.1) | copy-start | bytes 1572868
  0.7 7.7 %copy-start.8 = (bf16[84,512]{1,0:T(8,128)(2,1)S(1)}, bf16[84,512]{1,0:T(8,128)(2,1)}, u32[]{:S(2)}) copy-start(bf16[84,512]{1,0:T(8,128)(2,1)} %w_embed.1) | copy-start | bytes 258052
  0.7 7.7 %copy-start.9 = (bf16[512,84]{0,1:T(8,128)(2,1)S(1)}, bf16[512,84]{0,1:T(8,128)(2,1)}, u32[]{:S(2)}) copy-start(bf16[512,84]{0,1:T(8,128)(2,1)} %param.33) | copy-start | bytes 258052
  0.7 7.7 %copy-start.11 = (f32[512]{0:T(512)S(1)}, f32[512]{0:T(512)}, u32[]{:S(2)}) copy-start(f32[512]{0:T(512)} %param.22) | copy-start | bytes 6148
  0.7 7.7 %copy-start.12 = (f32[512]{0:T(512)S(1)}, f32[512]{0:T(512)}, u32[]{:S(2)}) copy-start(f32[512]{0:T(512)} %param.24) | copy-start | bytes 6148
  0.7 7.7 %copy-start.13 = (f32[512]{0:T(512)S(1)}, f32[512]{0:T(512)}, u32[]{:S(2)}) copy-start(f32[512]{0:T(512)} %param.25) | copy-start | bytes 6148
  0.8 7.7 %copy-start.14 = (f32[512]{0:T(512)S(1)}, f32[512]{0:T(512)}, u32[]{:S(2)}) copy-start(f32[512]{0:T(512)} %param.28) | copy-start | bytes 6148
  0.8 7.7 %copy-start.15 = (f32[512]{0:T(512)S(1)}, f32[512]{0:T(512)}, u32[]{:S(2)}) copy-start(f32[512]{0:T(512)} %param.32) | copy-start | bytes 6148
  2.3 15.1 %collective-permute-start = (bf16[176,640]{1,0:T(8,128)(2,1)S(1)}, bf16[176,640]{1,0:T(8,128)(2,1)S(1)}, u32[]{:S(2)}, u32[]{:S(2)}) collective-permute-start(bf16[176,640]{1,0:T(8,128)(2,1)S(1)} %get-tuple-element.17), channel_id=1, source_target_pairs={{0,2},{2,4},{4,6},{6,8},{8,10},{10,12},{12,14},{14,0},{1,3},{3,5},... | collective-permute-start | bytes 675848 | tf_op jit(solution)/shard_map/ppermute | solution.py:436
  5.3 12.1 %collective-permute-start.1 = (bf16[176,640]{1,0:T(8,128)(2,1)S(1)}, bf16[176,640]{1,0:T(8,128)(2,1)S(1)}, u32[]{:S(2)}, u32[]{:S(2)}) collective-permute-start(bf16[176,640]{1,0:T(8,128)(2,1)S(1)} %get-tuple-element.18), channel_id=1, source_target_pairs={{2,0},{4,2},{6,4},{8,6},{10,8},{12,10},{14,12},{0,14},{3,1},{5,3},... | collective-permute-start | bytes 675848 | tf_op jit(solution)/shard_map/ppermute | solution.py:437
  8.5 8.9 %copy-start.10 = (s32[2048,3]{0,1:T(4,128)S(1)}, s32[2048,3]{0,1:T(4,128)}, u32[]{:S(2)}) copy-start(s32[2048,3]{0,1:T(4,128)} %param.36) | copy-start | bytes 73732
  8.5 8.9 %copy-start.16 = (f32[84]{0:T(128)S(1)}, f32[84]{0:T(128)}, u32[]{:S(2)}) copy-start(f32[84]{0:T(128)} %param.34) | copy-start | bytes 1012
  17.4 15.4 %copy-start = (f32[2048,84]{0,1:T(8,128)S(1)}, f32[2048,84]{0,1:T(8,128)}, u32[]{:S(2)}) copy-start(f32[2048,84]{0,1:T(8,128)} %param.39) | copy-start | bytes 2064388
  17.4 15.4 %copy-start.1 = (bf16[2048,84]{0,1:T(8,128)(2,1)S(1)}, bf16[2048,84]{0,1:T(8,128)(2,1)}, u32[]{:S(2)}) copy-start(bf16[2048,84]{0,1:T(8,128)(2,1)} %param.38) | copy-start | bytes 1032196
  31.1 1.7 %collective-permute-start.2 = (bf16[84,2048]{1,0:T(8,128)(2,1)S(1)}, bf16[84,2048]{1,0:T(8,128)(2,1)S(1)}, u32[]{:S(2)}, u32[]{:S(2)}) collective-permute-start(bf16[84,2048]{1,0:T(8,128)(2,1)S(1)} %get-tuple-element.31.total_ref), channel_id=1, source_target_pairs={{0,1},{1,0},{2,3},{3,2},{4,5},{5,4},{6,7},{7,6},{8,9},{9,8},{10,11... | collective-permute-start | bytes 1032200 | tf_op jit(solution)/shard_map/ppermute | solution.py:496

commit v3 on v2

v3 whole, which is shorter than its diff:
```python
import functools

import jax
import jax.numpy as jnp
from jax import lax
from jax.experimental import pallas as pl
from jax.experimental.pallas import tpu as pltpu
from jax.sharding import PartitionSpec as P

REACH = 32
GRIM = 128
MHALO = 2 * REACH
EMPTY = -4096
F32 = jnp.float32
BF16 = jnp.bfloat16


def dot(a, b):
    return jnp.dot(a, b, preferred_element_type=F32)


def silu(u):
    return u + u * jnp.tanh(u)


def iota(shape, dim):
    return lax.broadcasted_iota(jnp.int32, shape, dim)


def ranks(shape, dim):
    return iota(shape, dim).astype(F32).astype(BF16)


def twice(a):
    return jnp.concatenate([a, a], axis=0)


def wide(a, width):
    return jnp.concatenate([a] * (width // a.shape[1]), axis=1)


def wrap(a, size):
    a = jnp.where(a < 0, a + size, a)
    return jnp.where(a >= size, a - size, a)


def small(idx):
    return idx.astype(F32).astype(BF16)


def marks(idx, height):
    rows = ranks((height, idx.shape[1]), 0)
    return jnp.where(rows == idx, jnp.ones((), BF16), jnp.zeros((), BF16))


def counts(idx, height, base):
    parts = []
    for first in range(0, height, 256):
        size = min(256, height - first)
        near = small(idx - (base + first))
        total = marks(near[0:1], size)
        for slot in range(1, idx.shape[0]):
            total = total + marks(near[slot : slot + 1], size)
        parts.append(total)
    return parts[0] if len(parts) == 1 else jnp.concatenate(parts, axis=0)


def spread(channels, members, member):
    shape = (channels * members, channels)
    return jnp.where(iota(shape, 0) == iota(shape, 1) * members + member, 1.0, 0.0).astype(BF16)


def turned(w, scale):
    return (w.astype(F32) * scale).T.astype(BF16)


def column(b, scale):
    return (jnp.broadcast_to(b, (128, b.shape[1])) * scale).T


def fetch(sources, targets, sems):
    copies = [
        pltpu.make_async_copy(source, target, sems.at[i])
        for i, (source, target) in enumerate(zip(sources, targets))
    ]
    for copy in copies:
        copy.start()
    return copies


def pack_kernel(
    patches,
    place,
    fields_hbm,
    senders_hbm,
    near_hbm,
    x_ref,
    up_ref,
    down_ref,
    k_ref,
    n_ref,
    fields_ref,
    senders_ref,
    near_ref,
    sems,
):
    channels, members, rows = fields_ref.shape
    kx = channels * members
    count = sems.shape[0] - 2
    cuts = [channels * i // count for i in range(count + 1)]
    cuts = [slice(a, b) for a, b in zip(cuts, cuts[1:])]
    copies = fetch(
        [senders_hbm, near_hbm] + [fields_hbm.at[cut] for cut in cuts],
        [senders_ref, near_ref] + [fields_ref.at[cut] for cut in cuts],
        sems,
    )
    for copy in copies[:2]:
        copy.wait()
    nodes = senders_ref.shape[1]
    nbrs = near_ref.shape[0]
    stride = rows // nodes
    halo = up_ref.shape[1]
    senders = senders_ref[...]
    node = iota(senders.shape, 1)
    k = wrap(senders - place[0] * rows - node * stride + GRIM, rows * patches) - GRIM
    k = jnp.where(senders >= 0, k, EMPTY)
    k = pltpu.roll(k, MHALO, 1)
    k_ref[...] = k
    near = near_ref[...]
    near = wrap(near - place[0] * nodes - iota(near.shape, 1) + REACH, nodes * patches) - REACH
    n_ref[:nbrs, :] = near
    n_ref[nbrs:, :] = jnp.zeros((8 - nbrs, nodes), jnp.int32)
    near = pltpu.roll(n_ref[...], MHALO, 1)
    n_ref[...] = near
    zero = jnp.zeros((8, halo - 3 * 128), F32)
    k = k.astype(F32)[:, :128]
    extra = [k[:8], k[8:], near.astype(F32)[:, :128], zero]
    extra = jnp.concatenate(extra, axis=1).astype(BF16)
    for copy in copies[2:]:
        copy.wait()
    x = fields_ref[...].reshape(kx, rows)
    x_ref[:kx, :] = x
    x_ref[kx:, :] = jnp.zeros((x_ref.shape[0] - kx, rows), BF16)
    up_ref[...] = jnp.concatenate([x[:, rows - halo :], extra], axis=0)
    down_ref[...] = jnp.concatenate([x[:, :halo], extra], axis=0)


def embed_rows(members, x_ref, w_embed, b_embed, h_ref, embed_t, col_ref):
    channels, hidden = w_embed.shape
    rows = x_ref.shape[1]
    kx = channels * members
    for m in range(members):
        sp = spread(channels, members, m)
        we = dot(sp, w_embed[...]) * 0.5
        we = jnp.concatenate([we, jnp.zeros((x_ref.shape[0] - kx, hidden), F32)], axis=0)
        embed_t[m * hidden : (m + 1) * hidden, :] = we.T.astype(BF16)
    col_ref[...] = column(b_embed[...], 0.5)
    pre = dot(embed_t[...], x_ref[...])
    h_ref[...] = silu((pre + wide(twice(col_ref[...]), rows)).astype(BF16))


def own_counts(k_ref, count_ref):
    rows, nodes = count_ref.shape
    stride = rows // nodes
    node = (iota(k_ref.shape, 1) + (nodes - MHALO)) % nodes
    idx = k_ref[...] + node * stride
    for base in range(0, rows, 128):
        near = small(idx - base)
        first = max(0, (base - GRIM - stride) // stride)
        last = min(nodes - 1, (base + 127 + GRIM) // stride)
        touched = {(r + MHALO) % nodes // 128 for r in range(first, last + 1)}
        for tile in range(nodes // 128):
            lanes = slice(128 * tile, 128 * (tile + 1))
            if tile in touched:
                total = marks(near[0:1, lanes], 128)
                for slot in range(1, idx.shape[0]):
                    total = total + marks(near[slot : slot + 1, lanes], 128)
            else:
                total = jnp.zeros((128, 128), BF16)
            count_ref[base : base + 128, lanes] = total


def early_kernel(members, place, down_in, x_ref, w_embed, b_embed, down_ref, *outs):
    del down_in, down_ref

    @pl.when(place[0] == 0)
    def _():
        embed_rows(members, x_ref, w_embed, b_embed, *outs)


def own_kernel(members, place, x_ref, w_embed, b_embed, *refs):
    k_ref, w_encode, w_decgrid = refs[3:6]
    b_encode, gain, w_receive, w_sender, b_process, w_update, w_decmesh, b_decode, w_output = refs[6:15]
    early = refs[15:18]
    gp_ref, edge_ref, part_ref, mesh_t, out_t, cols_ref, wcat, msg_ref, count_ref = refs[18:]
    h_ref = early[0]

    @pl.when(place[0] != 0)
    def _():
        embed_rows(members, x_ref, w_embed, b_embed, *early)

    own_counts(k_ref, count_ref)
    hidden = w_update.shape[0]
    rows = h_ref.shape[1]
    channels = w_output.shape[0]
    wcat[:hidden, :] = turned(w_encode[...], 0.5)
    wcat[hidden:, :] = turned(w_decgrid[...], 0.5)
    cols_ref[0] = column(b_encode[...], 0.5)
    cols_ref[1] = column(b_process[...], 0.5)
    cols_ref[2] = column(gain[...], 1.0)
    cols_ref[3] = column(b_decode[...], 0.5)
    for m in range(members):
        part = slice(m * hidden, (m + 1) * hidden)
        y = dot(wcat[...], h_ref[part, :])
        msg_ref[part, :] = silu((y[:hidden] + wide(cols_ref[0], rows)).astype(BF16))
        gp_ref[part, :] = (y[hidden:] + wide(cols_ref[3], rows)).astype(BF16)
    edge_ref[:, :GRIM] = msg_ref[:, :GRIM]
    edge_ref[:, GRIM:] = msg_ref[:, rows - GRIM :]
    part_ref[...] = dot(msg_ref[...], count_ref[...])
    for m in range(members):
        sp = spread(channels, members, m)
        out_t[:, m * hidden : (m + 1) * hidden] = dot(sp, w_output[...]).astype(BF16)
    mesh_t[0] = turned(w_sender[...], 0.5)
    mesh_t[1] = turned(w_receive[...], 0.5)
    mesh_t[2] = turned(w_update[...], 1.0)
    mesh_t[3] = turned(w_decmesh[...], 0.5)


def halo_messages(members, embed_t, wcat, col_ref, cols_ref, xh_ref, halo_ref, msg_ref):
    hidden = wcat.shape[1]
    top, halo = halo_ref.shape
    xh_ref[:top, :] = halo_ref[...]
    xh_ref[top:, :] = jnp.zeros((xh_ref.shape[0] - top, halo), BF16)
    h = silu((dot(embed_t[...], xh_ref[...]) + wide(twice(col_ref[...]), halo)).astype(BF16))
    for m in range(members):
        part = slice(m * hidden, (m + 1) * hidden)
        y = dot(wcat[:hidden, :], h[part])
        msg_ref[part, :] = silu((y + wide(cols_ref[0], halo)).astype(BF16))


def offsets(halo_ref):
    tail = halo_ref.shape[0] - 16
    sent = halo_ref[tail:, :].astype(F32)[8:].astype(jnp.int32)
    return jnp.concatenate([sent[:, :128], sent[:, 128:256]], axis=0), sent[:, 256:384]


def latent_rows(members, sums, gain):
    hidden = sums.shape[0] // members
    latents = []
    for m in range(members):
        s = sums[m * hidden : (m + 1) * hidden]
        scale = lax.rsqrt(jnp.sum(s * s, axis=0, keepdims=True) * (1.0 / hidden) + 1e-5)
        latents.append((wide(gain, sums.shape[1]) * s * scale).astype(BF16))
    return jnp.concatenate(latents, axis=1)


def stacked(members, a):
    lanes = a.shape[1] // members
    return jnp.concatenate([a[:, m * lanes : (m + 1) * lanes] for m in range(members)], axis=0)


def process_sum(window, at, base):
    height = window.shape[1]
    total = None
    for j in range(0, 6, 2):
        pair = jnp.concatenate([at[j : j + 1], at[j + 1 : j + 2]], axis=1)
        hot = [marks(small(pair - f), min(256, height - f)) for f in range(0, height, 256)]
        hot = hot[0] if len(hot) == 1 else jnp.concatenate(hot, axis=0)
        got = dot(window, hot).astype(BF16) + wide(base, 256)
        act = silu(got).astype(F32)
        act = act[:, :128] + act[:, 128:]
        total = act if total is None else total + act
    return total.astype(BF16)


def left_kernel(
    members,
    lo_ref,
    k_ref,
    near_ref,
    embed_t,
    col_ref,
    edge_ref,
    part_ref,
    mesh_t,
    cols_ref,
    wcat,
    latent_ref,
    send_ref,
    recv_ref,
    proc_ref,
    xh_ref,
    msg_ref,
):
    halo = lo_ref.shape[1]
    halo_messages(members, embed_t, wcat, col_ref, cols_ref, xh_ref, lo_ref, msg_ref)
    slots, lo_near = offsets(lo_ref)
    lane = iota(slots.shape, 1)
    near_by = lane * 8 + (halo - 8 * MHALO)
    own = near_by + k_ref[:, :128]
    left = jnp.where(lane < MHALO, near_by + slots, jnp.where(own < halo, own, EMPTY))
    lsum = dot(msg_ref[...], counts(left, halo, 0)) + dot(
        edge_ref[:, :GRIM], counts(left, GRIM, halo)
    )
    seam = part_ref[:, :128]
    lsum = lsum + jnp.where(iota(seam.shape, 1) >= MHALO, seam, 0.0)
    sums = jnp.concatenate([lsum, part_ref[:, 128:]], axis=1)
    latent = latent_rows(members, sums, cols_ref[2])
    latent_ref[...] = latent
    send_ref[...] = stacked(members, dot(mesh_t[0], latent).astype(BF16))
    recv = (dot(mesh_t[1], latent) + wide(cols_ref[1], latent.shape[1])).astype(BF16)
    recv_ref[...] = stacked(members, recv)
    seam = near_ref[:, :128]
    lane = iota(seam.shape, 1)
    at = jnp.where(lane < MHALO, lo_near, seam) + lane
    proc_ref[...] = process_sum(send_ref[...], at, recv_ref[:, :128])


def rest_kernel(
    members,
    patches,
    place,
    hi_ref,
    x_ref,
    k_ref,
    near_ref,
    sent_ref,
    embed_t,
    col_ref,
    gp_ref,
    edge_ref,
    part_ref,
    mesh_t,
    out_t,
    cols_ref,
    wcat,
    latent_ref,
    send_ref,
    recv_ref,
    proc_ref,
    bout_ref,
    pred_ref,
    total_ref,
    xh_ref,
    msg_ref,
    sr_ref,
    sum_ref,
    p_ref,
):
    hidden = wcat.shape[1]
    kx = out_t.shape[0]
    channels = kx // members
    rows = x_ref.shape[1]
    halo = hi_ref.shape[1]
    nodes = k_ref.shape[1]
    halo_messages(members, embed_t, wcat, col_ref, cols_ref, xh_ref, hi_ref, msg_ref)
    slots, hi_near = offsets(hi_ref)
    lane = iota(slots.shape, 1)
    near_by = lane * 8 - (rows - GRIM - 8 * (nodes - MHALO))
    own = near_by + k_ref[:, :128]
    right = jnp.where(lane >= MHALO, near_by + slots, jnp.where(own >= GRIM, own, EMPTY))
    rsum = dot(edge_ref[:, GRIM:], counts(right, GRIM, 0)) + dot(
        msg_ref[...], counts(right, halo, GRIM)
    )
    seam = part_ref[:, :128]
    rsum = rsum + jnp.where(iota(seam.shape, 1) < MHALO, seam, 0.0)
    latent = latent_rows(members, rsum, cols_ref[2])
    sr_ref[:, :256] = send_ref[...]
    sr_ref[:, 256:] = stacked(members, dot(mesh_t[0], latent).astype(BF16))
    recv = (dot(mesh_t[1], latent) + wide(cols_ref[1], latent.shape[1])).astype(BF16)
    seam = near_ref[:, :128]
    lane = iota(seam.shape, 1)
    mid = process_sum(sr_ref[...], near_ref[:, 128:] + lane + 128, recv_ref[:, 128:])
    at = jnp.where(lane >= MHALO, hi_near, seam) + lane + 128
    last = process_sum(sr_ref[:, 128:], at, stacked(members, recv))
    sums = [proc_ref[...], mid, last]
    pieces = [s[m * hidden : (m + 1) * hidden] for m in range(members) for s in sums]
    process = jnp.concatenate(pieces, axis=1)
    pieces = []
    for m in range(members):
        pieces.append(latent_ref[:, 256 * m : 256 * (m + 1)])
        pieces.append(latent[:, 128 * m : 128 * (m + 1)])
    latent = jnp.concatenate(pieces, axis=1)
    new = (latent.astype(F32) + dot(mesh_t[2], process)).astype(BF16)
    sr_ref[...] = stacked(members, dot(mesh_t[3], new).astype(BF16))
    sent = wrap(sent_ref[...] - place[0] * nodes + MHALO, nodes * patches)
    half = rows // 2
    idx = small(jnp.where(iota(sent.shape, 1) >= half, sent - 128, sent))
    for b in range(2):
        lanes = slice(b * half, (b + 1) * half)
        window = sr_ref[:, 128 * b : 128 * b + 256]
        total = None
        for j in range(idx.shape[0]):
            got = dot(window, marks(idx[j : j + 1, lanes], 256)).astype(BF16)
            act = silu(got + gp_ref[:, lanes])
            total = act if total is None else total + act
        sum_ref[:, lanes] = total
    bout = (iota((kx, channels), 0) // members == iota((kx, channels), 1)).astype(F32)
    bout = jnp.sum(bout * bout_ref[...], axis=1, keepdims=True)
    delta = dot(out_t[...], sum_ref[...]) + bout
    pred = (x_ref[:kx, :].astype(F32) + delta).astype(BF16)
    pred_ref[...] = pred.reshape(channels, members, rows)
    p_ref[:kx, :] = pred
    p_ref[kx:, :] = jnp.zeros((p_ref.shape[0] - kx, rows), BF16)
    shape = (channels, x_ref.shape[0])
    fold = jnp.where(iota(shape, 1) // members == iota(shape, 0), 1.0, 0.0).astype(BF16)
    total_ref[...] = dot(fold, p_ref[...]).astype(BF16)


def week_kernel(count, total_ref, other_ref, week_ref, clim_ref, out_ref):
    ensemble = (total_ref[...].astype(F32) + other_ref[...].astype(F32)) * (1.0 / count)
    out_ref[...] = week_ref[...] + ensemble - clim_ref[...].astype(F32)


def call(kernel, outs, scratch, name, args, flops, spaces, limit=24, aliases={}):
    kinds = {"s": pltpu.SMEM, "v": pltpu.VMEM, "h": pltpu.HBM, "f": pltpu.VMEM}
    args = [
        a if kind in "sf" else pltpu.with_memory_space_constraint(a, kinds[kind])
        for a, kind in zip(args, spaces, strict=True)
    ]
    return pl.pallas_call(
        kernel,
        out_shape=outs,
        in_specs=[pl.BlockSpec(memory_space=kinds[kind]) for kind in spaces],
        out_specs=[pl.BlockSpec(memory_space=pltpu.VMEM)] * len(outs),
        scratch_shapes=scratch,
        name=name,
        input_output_aliases=aliases,
        compiler_params=pltpu.CompilerParams(vmem_limit_bytes=limit * 1024 * 1024),
        cost_estimate=pl.CostEstimate(flops=flops, bytes_accessed=1 << 22, transcendentals=0),
    )(*args)


def shards(
    fields,
    w_embed,
    b_embed,
    w_encode,
    b_encode,
    mesh_gain,
    w_receive,
    w_sender,
    b_process,
    w_update,
    w_decmesh,
    w_decgrid,
    b_decode,
    w_output,
    b_output,
    g2m_senders,
    m2g_senders,
    mesh_neighbours,
    climatology,
    week_sum,
):
    members, rows, channels = fields.shape
    hidden = w_encode.shape[0]
    nodes, nbrs = mesh_neighbours.shape
    slots = g2m_senders.shape[1]
    patches = lax.axis_size("patch")
    place = lax.axis_index("patch").astype(jnp.int32).reshape(1)
    kx = members * channels
    kpad = -(-kx // 256) * 256
    halo = MHALO * (rows // nodes) + GRIM
    ext = nodes + 2 * MHALO
    shape = jax.ShapeDtypeStruct
    inside = pltpu.VMEM

    args = (jnp.transpose(fields, (2, 0, 1)), g2m_senders.T, mesh_neighbours.T)
    x, from_low, from_high, k, near = call(
        functools.partial(pack_kernel, patches),
        [
            inside((kpad, rows), BF16),
            inside((kx + 8, halo), BF16),
            inside((kx + 8, halo), BF16),
            inside((slots, nodes), jnp.int32),
            inside((8, nodes), jnp.int32),
        ],
        [pltpu.VMEM(a.shape, a.dtype) for a in args] + [pltpu.SemaphoreType.DMA((3,))],
        "pack_halo",
        (place,) + args,
        2 * 10**10,
        "shhh",
    )
    up = [(i, (i + 1) % patches) for i in range(patches)]
    down = [(target, source) for source, target in up]
    lo = lax.ppermute(from_low, "patch", up)
    embedded = [
        inside((members * hidden, rows), BF16),
        inside((members * hidden, kpad), BF16),
        inside((hidden, 128), F32),
    ]
    args = (x, w_embed, b_embed[None])
    from_high, *early = call(
        functools.partial(early_kernel, members),
        [inside((kx + 8, halo), BF16)] + embedded,
        [],
        "embed_early",
        (place, from_high) + args,
        10**10,
        "svvff",
        20,
        {1: 0},
    )
    hi = lax.ppermute(from_high, "patch", down)
    own = call(
        functools.partial(own_kernel, members),
        embedded
        + [
            inside((members * hidden, rows), BF16),
            inside((members * hidden, 2 * GRIM), BF16),
            inside((members * hidden, nodes), F32),
            inside((4, hidden, hidden), BF16),
            inside((kx, members * hidden), BF16),
            inside((4, hidden, 128), F32),
            inside((2 * hidden, hidden), BF16),
        ],
        [pltpu.VMEM((members * hidden, rows), BF16), pltpu.VMEM((rows, nodes), BF16)],
        "own_rows",
        (place,)
        + args
        + tuple(early)
        + (
            k,
            w_encode,
            w_decgrid,
            b_encode[None],
            mesh_gain[None],
            w_receive,
            w_sender,
            b_process[None],
            w_update,
            w_decmesh,
            b_decode[None],
            w_output.T,
        ),
        10**10,
        "svff" + "vvv" + "v" + "f" * 11,
        28,
        {4 + i: i for i in range(3)},
    )
    embed_t, col = own[1:3]
    own = own[3:]
    gp, edge, part, mesh_t, out_t, cols, wcat = own
    halo_scratch = [pltpu.VMEM((kpad, halo), BF16), pltpu.VMEM((members * hidden, halo), BF16)]
    left = call(
        functools.partial(left_kernel, members),
        [
            inside((hidden, members * 256), BF16),
            inside((members * hidden, 256), BF16),
            inside((members * hidden, 256), BF16),
            inside((members * hidden, 128), BF16),
        ],
        halo_scratch,
        "low_side",
        (lo, k, near, embed_t, col, edge, part, mesh_t, cols, wcat),
        10**10,
        "v" * 10,
        20,
    )
    pred, total = call(
        functools.partial(rest_kernel, members, patches),
        [inside((channels, members, rows), BF16), inside((channels, rows), BF16)],
        halo_scratch
        + [
            pltpu.VMEM((members * hidden, ext), BF16),
            pltpu.VMEM((members * hidden, rows), BF16),
            pltpu.VMEM((kpad, rows), BF16),
        ],
        "high_side_decode",
        (place, hi, x, k, near, m2g_senders.T, embed_t, col)
        + tuple(own)
        + tuple(left)
        + (b_output[None],),
        2 * 10**10,
        "s" + "v" * 19,
        32,
    )
    prediction = jnp.transpose(pred, (1, 2, 0))
    other = lax.ppermute(total, "member", [(0, 1), (1, 0)])
    (week_total,) = call(
        functools.partial(week_kernel, members * lax.axis_size("member")),
        [shape((channels, rows), F32)],
        [],
        "week",
        (total, other, week_sum.T, climatology.T),
        10**6,
        "vvvv",
    )
    return (prediction, week_total.T)


def solution(mesh):
    grid = P(("groups", "member"), "patch", None)
    node = P("patch", None)
    week = P(("groups", "patch"), None)
    return jax.shard_map(
        shards,
        mesh=mesh,
        in_specs=(grid,) + (P(),) * 14 + (node,) * 4 + (week,),
        out_specs=(grid, week),
        check_vma=False,
    )
```

time: 34 us -> 33 us (0.971)
  starting transfers between devices: 6.17 us -> 4.46 us
  Pallas kernels: 25 us -> 25.7 us
    ppermute x1, starting transfers between devices: 3.1 us -> 1.4 us  [shards(): hi = lax.ppermute(from_high, 'patch', down)]
    pallas_call x4 -> x6, Pallas kernels: 25 us -> 25.7 us  [call(): pl.pallas_call(kernel, out_shape=outs, in_specs=[pl.BlockSpec(memory_spac...]
  transfers between devices with their start and end apart: 3 -> 3, of which waited for: 1 -> 1; matrix products, arithmetic and copies ran while one was open for 3% -> 3% of each run, Pallas kernels for 26% -> 38%
where the time goes in v3:
time: 33 us; the launch traced here: 32.8 us
  Pallas kernels  25.7 us (78%)
  starting transfers between devices  4.46 us (14%)
  local copies, waits for them, and re-layouts  0.95 us (3%)
  between operations  0.9 us (3%)
  waiting for transfers between devices  0.82 us (2%)
    pallas_call x6, Pallas kernels, call(): pl.pallas_call(kernel, out_shape=outs, in_specs=[pl.BlockSpec(memory_spac...  25.7 us
    ppermute x1, starting transfers between devices, shards(): lo = lax.ppermute(from_low, 'patch', up)  2.99 us
    ppermute x1, starting transfers between devices, shards(): hi = lax.ppermute(from_high, 'patch', down)  1.4 us
    unnamed x35, local copies, waits for them, and re-layouts  0.95 us
    ppermute x1, waiting for transfers between devices, shards(): other = lax.ppermute(total, 'member', [(0, 1), (1, 0)])  0.81 us
  transfers between devices with their start and end apart: 3, of which 1 were waited for; matrix products, arithmetic and copies ran while one was open for 3% of the time, Pallas kernels for 38%

profile of v3, /device:TPU:0, one launch (start us, length us, event | category | flops | bytes accessed | tf_op | source)
XLA Modules:
  0.0 32.8 jit_solution(18445192302387205215)
XLA Ops:
  0.6 0.0 copy-start.8
  0.6 0.0 copy-start.11
  0.7 1.4 %pack_halo.1 = (bf16[256,2048]{1,0:T(8,128)(2,1)S(1)}, bf16[176,640]{1,0:T(8,128)(2,1)S(1)}, bf16[176,640]{1,0:T(8,128)(2,1)S(1)}, s32[16,256]{1,0:T(8,128)S(1)}, s32[8,256]{1,0:T(8,128)S(1)}) custom-call(s32[1]{0:T(128)} %bitcast.place, bf16[84,2,2048]{2,1,0:T(2,128)(2,1)} %bitcast.29, s32[16,256]{1,0:T(8,128)} %bitcast.30, s32[6,256]{1,0:T(8,128)} %bitcast.31), custom_call_target="tpu_custom_call" | custom-call | flops 20000000000 | bytes 4194304 | tf_op jit(solution)/shard_map/pack_halo/pallas_call | solution.py:421
  2.1 3.0 %collective-permute-start.1 = (bf16[176,640]{1,0:T(8,128)(2,1)S(1)}, bf16[176,640]{1,0:T(8,128)(2,1)S(1)}, u32[]{:S(2)}, u32[]{:S(2)}) collective-permute-start(bf16[176,640]{1,0:T(8,128)(2,1)S(1)} %get-tuple-element.43), channel_id=1, source_target_pairs={{0,2},{2,4},{4,6},{6,8},{8,10},{10,12},{12,14},{14,0},{1,3},{3,5},... | collective-permute-start | bytes 675848 | tf_op jit(solution)/shard_map/ppermute | solution.py:487
  5.1 0.0 copy-done.8
  5.1 0.0 copy-done.11
  5.1 0.0 copy-start.2
  5.1 0.0 copy-start.3
  5.1 0.0 copy-start.4
  5.1 0.0 copy-start.5
  5.1 0.0 copy-start.6
  5.1 0.0 copy-start.7
  5.1 0.0 copy-start.9
  5.1 0.0 copy-start.12
  5.1 0.0 copy-start.13
  5.2 0.0 copy-start.14
  5.2 0.0 copy-start.15
  5.2 1.7 %embed_early.1 = (bf16[176,640]{1,0:T(8,128)(2,1)S(1)}, bf16[1024,2048]{1,0:T(8,128)(2,1)S(1)}, bf16[1024,256]{1,0:T(8,128)(2,1)S(1)}, f32[512,128]{1,0:T(8,128)S(1)}) custom-call(s32[1]{0:T(128)} %bitcast.place, bf16[176,640]{1,0:T(8,128)(2,1)S(1)} %get-tuple-element.26.down_in, ...), custom_call_target="tpu_custom_call", output_to_operand_aliasing={{0}: (1, {})} | custom-call | flops 10000000000 | bytes 4194304 | tf_op jit(solution)/shard_map/embed_early/pallas_call | solution.py:421
  6.9 1.4 %collective-permute-start = (bf16[176,640]{1,0:T(8,128)(2,1)S(1)}, bf16[176,640]{1,0:T(8,128)(2,1)S(1)}, u32[]{:S(2)}, u32[]{:S(2)}) collective-permute-start(bf16[176,640]{1,0:T(8,128)(2,1)S(1)} %get-tuple-element.28), channel_id=1, source_target_pairs={{2,0},{4,2},{6,4},{8,6},{10,8},{12,10},{14,12},{0,14},{3,1},{5,3},... | collective-permute-start | bytes 675848 | tf_op jit(solution)/shard_map/ppermute | solution.py:505
  8.3 0.0 copy-done.2
  8.3 0.0 copy-done.3
  8.3 0.0 copy-done.4
  8.3 0.0 copy-done.5
  8.3 0.0 copy-done.6
  8.4 0.0 copy-done.7
  8.4 0.0 copy-done.9
  8.4 0.0 copy-done.12
  8.4 0.0 copy-done.13
  8.4 0.0 copy-done.14
  8.4 0.0 copy-done.15
  8.4 7.0 %own_rows.1 = (bf16[1024,2048]{1,0:T(8,128)(2,1)S(1)}, bf16[1024,256]{1,0:T(8,128)(2,1)S(1)}, f32[512,128]{1,0:T(8,128)S(1)}, bf16[1024,2048]{1,0:T(8,128)(2,1)S...) custom-call(s32[1]{0:T(128)} %bitcast.place, ...), custom_call_target="tpu_custom_call", output_to_operand_aliasing={{0}: (4, {}), {1}: (5, {}), {2}: (6, {})} | custom-call | flops 10000000000 | bytes 4194304 | tf_op jit(solution)/shard_map/own_rows/pallas_call | solution.py:421
  15.4 0.0 collective-permute-done.1.lo_ref
  15.4 0.0 copy-start.10
  15.4 0.0 copy-start.16
  15.4 3.6 %low_side.1 = (bf16[512,512]{1,0:T(8,128)(2,1)S(1)}, bf16[1024,256]{1,0:T(8,128)(2,1)S(1)}, bf16[1024,256]{1,0:T(8,128)(2,1)S(1)}, bf16[1024,128]{1,0:T(8,128)(2,1)S(1)}) custom-call(bf16[176,640]{1,0:T(8,128)(2,1)S(1)} %collective-permute-done.1.lo_ref, s32[16,256]{1,0:T(8,128)S(1)} %get-tuple-element.29.refs_3_.k_ref, ...), custom_call_target="tpu_custom_call" | custom-call | flops 10000000000 | bytes 4194304 | tf_op jit(solution)/shard_map/low_side/pallas_call | solution.py:421
  19.1 0.0 collective-permute-done.hi_ref
  19.1 0.0 copy-done.10
  19.1 0.0 copy-done.16
  19.1 0.0 copy-start
  19.1 0.0 copy-start.1
  19.1 10.9 %high_side_decode.1 = (bf16[84,2,2048]{2,1,0:T(2,128)(2,1)S(1)}, bf16[84,2048]{1,0:T(8,128)(2,1)S(1)}) custom-call(s32[1]{0:T(128)} %bitcast.place, bf16[176,640]{1,0:T(8,128)(2,1)S(1)} %collective-permute-done.hi_ref, bf16[256,2048]{1,0:T(8,128)(2,1)S(1)} %get-tuple-element.27.x_ref, s32[16,256]{1,0:T(8,128)S(1)} %get-tuple-element.29.refs_3_.k_ref, ...), custom_call_target="tpu_custom_call" | custom-call | flops 20000000000 | bytes 4194304 | tf_op jit(solution)/shard_map/high_side_decode/pallas_call | solution.py:421
  30.1 0.1 collective-permute-start.2
  30.1 0.8 %copy.30 = bf16[2,2048,84]{1,0,2:T(2,128)(2,1)} copy(bf16[2,2048,84]{1,0,2:T(2,128)(2,1)S(1)} %bitcast.16) | data formatting | bytes 1376256
  31.0 0.8 %collective-permute-done.2.other_ref = bf16[84,2048]{1,0:T(8,128)(2,1)S(1)} collective-permute-done((bf16[84,2048]{1,0:T(8,128)(2,1)S(1)}, bf16[84,2048]{1,0:T(8,128)(2,1)S(1)}, u32[]{:S(2)}, u32[]{:S(2)}) %collective-permute-start.2) | collective-permute-done | bytes 344096 | tf_op jit(solution)/shard_map/ppermute | solution.py:580
  31.8 0.0 copy-done
  31.8 0.0 copy-done.1
  31.8 1.0 %week.1 = f32[84,2048]{1,0:T(8,128)} custom-call(bf16[84,2048]{1,0:T(8,128)(2,1)S(1)} %get-tuple-element.49.total_ref, bf16[84,2048]{1,0:T(8,128)(2,1)S(1)} %collective-permute-done.2.other_ref, f32[84,2048]{1,0:T(8,128)S(1)} %bitcast.17, bf16[84,2048]{1,0:T(8,128)(2,1)S(1)} %bitcast.18), custom_call_target="tpu_custom_call" | custom-call | flops 1000000 | bytes 4194304 | tf_op jit(solution)/shard_map/week/pallas_call | solution.py:421
Async XLA Ops:
  0.6 4.4 %copy-start.8 = (bf16[84,512]{1,0:T(8,128)(2,1)S(1)}, bf16[84,512]{1,0:T(8,128)(2,1)}, u32[]{:S(2)}) copy-start(bf16[84,512]{1,0:T(8,128)(2,1)} %w_embed.3) | copy-start | bytes 258052
  0.6 4.4 %copy-start.11 = (f32[512]{0:T(512)S(1)}, f32[512]{0:T(512)}, u32[]{:S(2)}) copy-start(f32[512]{0:T(512)} %param.22) | copy-start | bytes 6148
  2.1 13.3 %collective-permute-start.1 = (bf16[176,640]{1,0:T(8,128)(2,1)S(1)}, bf16[176,640]{1,0:T(8,128)(2,1)S(1)}, u32[]{:S(2)}, u32[]{:S(2)}) collective-permute-start(bf16[176,640]{1,0:T(8,128)(2,1)S(1)} %get-tuple-element.43), channel_id=1, source_target_pairs={{0,2},{2,4},{4,6},{6,8},{8,10},{10,12},{12,14},{14,0},{1,3},{3,5},... | collective-permute-start | bytes 675848 | tf_op jit(solution)/shard_map/ppermute | solution.py:487
  5.1 3.3 %copy-start.2 = (bf16[512,512]{1,0:T(8,128)(2,1)S(1)}, bf16[512,512]{1,0:T(8,128)(2,1)}, u32[]{:S(2)}) copy-start(bf16[512,512]{1,0:T(8,128)(2,1)} %refs_4_.1) | copy-start | bytes 1572868
  5.1 3.3 %copy-start.3 = (bf16[512,512]{1,0:T(8,128)(2,1)S(1)}, bf16[512,512]{1,0:T(8,128)(2,1)}, u32[]{:S(2)}) copy-start(bf16[512,512]{1,0:T(8,128)(2,1)} %refs_5_.1) | copy-start | bytes 1572868
  5.1 3.3 %copy-start.4 = (bf16[512,512]{1,0:T(8,128)(2,1)S(1)}, bf16[512,512]{1,0:T(8,128)(2,1)}, u32[]{:S(2)}) copy-start(bf16[512,512]{1,0:T(8,128)(2,1)} %refs_8_.1) | copy-start | bytes 1572868
  5.1 3.3 %copy-start.5 = (bf16[512,512]{1,0:T(8,128)(2,1)S(1)}, bf16[512,512]{1,0:T(8,128)(2,1)}, u32[]{:S(2)}) copy-start(bf16[512,512]{1,0:T(8,128)(2,1)} %refs_9_.1) | copy-start | bytes 1572868
  5.1 3.3 %copy-start.6 = (bf16[512,512]{1,0:T(8,128)(2,1)S(1)}, bf16[512,512]{1,0:T(8,128)(2,1)}, u32[]{:S(2)}) copy-start(bf16[512,512]{1,0:T(8,128)(2,1)} %refs_11_.1) | copy-start | bytes 1572868
  5.1 3.3 %copy-start.7 = (bf16[512,512]{1,0:T(8,128)(2,1)S(1)}, bf16[512,512]{1,0:T(8,128)(2,1)}, u32[]{:S(2)}) copy-start(bf16[512,512]{1,0:T(8,128)(2,1)} %refs_12_.1) | copy-start | bytes 1572868
  5.1 3.2 %copy-start.9 = (bf16[512,84]{0,1:T(8,128)(2,1)S(1)}, bf16[512,84]{0,1:T(8,128)(2,1)}, u32[]{:S(2)}) copy-start(bf16[512,84]{0,1:T(8,128)(2,1)} %param.33) | copy-start | bytes 258052
  5.1 3.2 %copy-start.12 = (f32[512]{0:T(512)S(1)}, f32[512]{0:T(512)}, u32[]{:S(2)}) copy-start(f32[512]{0:T(512)} %param.24) | copy-start | bytes 6148
  5.1 3.2 %copy-start.13 = (f32[512]{0:T(512)S(1)}, f32[512]{0:T(512)}, u32[]{:S(2)}) copy-start(f32[512]{0:T(512)} %param.25) | copy-start | bytes 6148
  5.2 3.2 %copy-start.14 = (f32[512]{0:T(512)S(1)}, f32[512]{0:T(512)}, u32[]{:S(2)}) copy-start(f32[512]{0:T(512)} %param.28) | copy-start | bytes 6148
  5.2 3.2 %copy-start.15 = (f32[512]{0:T(512)S(1)}, f32[512]{0:T(512)}, u32[]{:S(2)}) copy-start(f32[512]{0:T(512)} %param.32) | copy-start | bytes 6148
  6.9 12.1 %collective-permute-start = (bf16[176,640]{1,0:T(8,128)(2,1)S(1)}, bf16[176,640]{1,0:T(8,128)(2,1)S(1)}, u32[]{:S(2)}, u32[]{:S(2)}) collective-permute-start(bf16[176,640]{1,0:T(8,128)(2,1)S(1)} %get-tuple-element.28), channel_id=1, source_target_pairs={{2,0},{4,2},{6,4},{8,6},{10,8},{12,10},{14,12},{0,14},{3,1},{5,3},... | collective-permute-start | bytes 675848 | tf_op jit(solution)/shard_map/ppermute | solution.py:505
  15.4 3.7 %copy-start.10 = (s32[2048,3]{0,1:T(4,128)S(1)}, s32[2048,3]{0,1:T(4,128)}, u32[]{:S(2)}) copy-start(s32[2048,3]{0,1:T(4,128)} %param.36) | copy-start | bytes 73732
  15.4 3.7 %copy-start.16 = (f32[84]{0:T(128)S(1)}, f32[84]{0:T(128)}, u32[]{:S(2)}) copy-start(f32[84]{0:T(128)} %param.34) | copy-start | bytes 1012
  19.1 12.7 %copy-start = (f32[2048,84]{0,1:T(8,128)S(1)}, f32[2048,84]{0,1:T(8,128)}, u32[]{:S(2)}) copy-start(f32[2048,84]{0,1:T(8,128)} %param.39) | copy-start | bytes 2064388
  19.1 12.7 %copy-start.1 = (bf16[2048,84]{0,1:T(8,128)(2,1)S(1)}, bf16[2048,84]{0,1:T(8,128)(2,1)}, u32[]{:S(2)}) copy-start(bf16[2048,84]{0,1:T(8,128)(2,1)} %param.38) | copy-start | bytes 1032196
  30.1 1.7 %collective-permute-start.2 = (bf16[84,2048]{1,0:T(8,128)(2,1)S(1)}, bf16[84,2048]{1,0:T(8,128)(2,1)S(1)}, u32[]{:S(2)}, u32[]{:S(2)}) collective-permute-start(bf16[84,2048]{1,0:T(8,128)(2,1)S(1)} %get-tuple-element.49.total_ref), channel_id=1, source_target_pairs={{0,1},{1,0},{2,3},{3,2},{4,5},{5,4},{6,7},{7,6},{8,9},{9,8},{10,11... | collective-permute-start | bytes 1032200 | tf_op jit(solution)/shard_map/ppermute | solution.py:580

commit v4 on v3

--- a/solution.py
+++ b/solution.py
@@ -199,7 +199,6 @@
     def _():
         embed_rows(members, x_ref, w_embed, b_embed, *early)
 
-    own_counts(k_ref, count_ref)
     hidden = w_update.shape[0]
     rows = h_ref.shape[1]
     channels = w_output.shape[0]
@@ -212,18 +211,17 @@
     for m in range(members):
         part = slice(m * hidden, (m + 1) * hidden)
         y = dot(wcat[...], h_ref[part, :])
+        mesh_t[2 * m] = turned((w_sender, w_update)[m][...], (0.5, 1.0)[m])
+        mesh_t[2 * m + 1] = turned((w_receive, w_decmesh)[m][...], 0.5)
         msg_ref[part, :] = silu((y[:hidden] + wide(cols_ref[0], rows)).astype(BF16))
         gp_ref[part, :] = (y[hidden:] + wide(cols_ref[3], rows)).astype(BF16)
     edge_ref[:, :GRIM] = msg_ref[:, :GRIM]
     edge_ref[:, GRIM:] = msg_ref[:, rows - GRIM :]
+    own_counts(k_ref, count_ref)
     part_ref[...] = dot(msg_ref[...], count_ref[...])
     for m in range(members):
         sp = spread(channels, members, m)
         out_t[:, m * hidden : (m + 1) * hidden] = dot(sp, w_output[...]).astype(BF16)
-    mesh_t[0] = turned(w_sender[...], 0.5)
-    mesh_t[1] = turned(w_receive[...], 0.5)
-    mesh_t[2] = turned(w_update[...], 1.0)
-    mesh_t[3] = turned(w_decmesh[...], 0.5)
 
 
 def halo_messages(members, embed_t, wcat, col_ref, cols_ref, xh_ref, halo_ref, msg_ref):

time: 33 us -> 33 us (level)
  no operation moved by 1% of the time
where the time goes in v4:
time: 33 us; the launch traced here: 32.8 us
  Pallas kernels  25.7 us (78%)
  starting transfers between devices  4.46 us (14%)
  local copies, waits for them, and re-layouts  0.95 us (3%)
  between operations  0.9 us (3%)
  waiting for transfers between devices  0.82 us (2%)
    pallas_call x6, Pallas kernels, call(): pl.pallas_call(kernel, out_shape=outs, in_specs=[pl.BlockSpec(memory_spac...  25.7 us
    ppermute x1, starting transfers between devices, shards(): lo = lax.ppermute(from_low, 'patch', up)  2.99 us
    ppermute x1, starting transfers between devices, shards(): hi = lax.ppermute(from_high, 'patch', down)  1.4 us
    unnamed x35, local copies, waits for them, and re-layouts  0.95 us
    ppermute x1, waiting for transfers between devices, shards(): other = lax.ppermute(total, 'member', [(0, 1), (1, 0)])  0.81 us
  transfers between devices with their start and end apart: 3, of which 1 were waited for; matrix products, arithmetic and copies ran while one was open for 3% of the time, Pallas kernels for 38%

profile of v4, /device:TPU:0, one launch (start us, length us, event | category | flops | bytes accessed | tf_op | source)
XLA Modules:
  0.0 32.8 jit_solution(18445192302387205215)
XLA Ops:
  0.6 0.0 copy-start.8
  0.6 0.0 copy-start.11
  0.7 1.4 %pack_halo.1 = (bf16[256,2048]{1,0:T(8,128)(2,1)S(1)}, bf16[176,640]{1,0:T(8,128)(2,1)S(1)}, bf16[176,640]{1,0:T(8,128)(2,1)S(1)}, s32[16,256]{1,0:T(8,128)S(1)}, s32[8,256]{1,0:T(8,128)S(1)}) custom-call(s32[1]{0:T(128)} %bitcast.place, bf16[84,2,2048]{2,1,0:T(2,128)(2,1)} %bitcast.29, s32[16,256]{1,0:T(8,128)} %bitcast.30, s32[6,256]{1,0:T(8,128)} %bitcast.31), custom_call_target="tpu_custom_call" | custom-call | flops 20000000000 | bytes 4194304 | tf_op jit(solution)/shard_map/pack_halo/pallas_call | solution.py:419
  2.1 3.0 %collective-permute-start.1 = (bf16[176,640]{1,0:T(8,128)(2,1)S(1)}, bf16[176,640]{1,0:T(8,128)(2,1)S(1)}, u32[]{:S(2)}, u32[]{:S(2)}) collective-permute-start(bf16[176,640]{1,0:T(8,128)(2,1)S(1)} %get-tuple-element.43), channel_id=1, source_target_pairs={{0,2},{2,4},{4,6},{6,8},{8,10},{10,12},{12,14},{14,0},{1,3},{3,5},... | collective-permute-start | bytes 675848 | tf_op jit(solution)/shard_map/ppermute | solution.py:485
  5.1 0.0 copy-done.8
  5.1 0.0 copy-done.11
  5.1 0.0 copy-start.2
  5.1 0.0 copy-start.3
  5.1 0.0 copy-start.4
  5.1 0.0 copy-start.5
  5.1 0.0 copy-start.6
  5.1 0.0 copy-start.7
  5.1 0.0 copy-start.9
  5.1 0.0 copy-start.12
  5.1 0.0 copy-start.13
  5.2 0.0 copy-start.14
  5.2 0.0 copy-start.15
  5.2 1.7 %embed_early.1 = (bf16[176,640]{1,0:T(8,128)(2,1)S(1)}, bf16[1024,2048]{1,0:T(8,128)(2,1)S(1)}, bf16[1024,256]{1,0:T(8,128)(2,1)S(1)}, f32[512,128]{1,0:T(8,128)S(1)}) custom-call(s32[1]{0:T(128)} %bitcast.place, bf16[176,640]{1,0:T(8,128)(2,1)S(1)} %get-tuple-element.26.down_in, ...), custom_call_target="tpu_custom_call", output_to_operand_aliasing={{0}: (1, {})} | custom-call | flops 10000000000 | bytes 4194304 | tf_op jit(solution)/shard_map/embed_early/pallas_call | solution.py:419
  6.9 1.4 %collective-permute-start = (bf16[176,640]{1,0:T(8,128)(2,1)S(1)}, bf16[176,640]{1,0:T(8,128)(2,1)S(1)}, u32[]{:S(2)}, u32[]{:S(2)}) collective-permute-start(bf16[176,640]{1,0:T(8,128)(2,1)S(1)} %get-tuple-element.28), channel_id=1, source_target_pairs={{2,0},{4,2},{6,4},{8,6},{10,8},{12,10},{14,12},{0,14},{3,1},{5,3},... | collective-permute-start | bytes 675848 | tf_op jit(solution)/shard_map/ppermute | solution.py:503
  8.3 0.0 copy-done.2
  8.3 0.0 copy-done.3
  8.3 0.0 copy-done.4
  8.3 0.0 copy-done.5
  8.3 0.0 copy-done.6
  8.4 0.0 copy-done.7
  8.4 0.0 copy-done.9
  8.4 0.0 copy-done.12
  8.4 0.0 copy-done.13
  8.4 0.0 copy-done.14
  8.4 0.0 copy-done.15
  8.4 7.0 %own_rows.1 = (bf16[1024,2048]{1,0:T(8,128)(2,1)S(1)}, bf16[1024,256]{1,0:T(8,128)(2,1)S(1)}, f32[512,128]{1,0:T(8,128)S(1)}, bf16[1024,2048]{1,0:T(8,128)(2,1)S...) custom-call(s32[1]{0:T(128)} %bitcast.place, ...), custom_call_target="tpu_custom_call", output_to_operand_aliasing={{0}: (4, {}), {1}: (5, {}), {2}: (6, {})} | custom-call | flops 10000000000 | bytes 4194304 | tf_op jit(solution)/shard_map/own_rows/pallas_call | solution.py:419
  15.4 0.0 collective-permute-done.1.lo_ref
  15.4 0.0 copy-start.10
  15.4 0.0 copy-start.16
  15.4 3.6 %low_side.1 = (bf16[512,512]{1,0:T(8,128)(2,1)S(1)}, bf16[1024,256]{1,0:T(8,128)(2,1)S(1)}, bf16[1024,256]{1,0:T(8,128)(2,1)S(1)}, bf16[1024,128]{1,0:T(8,128)(2,1)S(1)}) custom-call(bf16[176,640]{1,0:T(8,128)(2,1)S(1)} %collective-permute-done.1.lo_ref, s32[16,256]{1,0:T(8,128)S(1)} %get-tuple-element.29.refs_3_.k_ref, ...), custom_call_target="tpu_custom_call" | custom-call | flops 10000000000 | bytes 4194304 | tf_op jit(solution)/shard_map/low_side/pallas_call | solution.py:419
  19.1 0.0 collective-permute-done.hi_ref
  19.1 0.0 copy-done.10
  19.1 0.0 copy-done.16
  19.1 0.0 copy-start
  19.1 0.0 copy-start.1
  19.1 10.9 %high_side_decode.1 = (bf16[84,2,2048]{2,1,0:T(2,128)(2,1)S(1)}, bf16[84,2048]{1,0:T(8,128)(2,1)S(1)}) custom-call(s32[1]{0:T(128)} %bitcast.place, bf16[176,640]{1,0:T(8,128)(2,1)S(1)} %collective-permute-done.hi_ref, bf16[256,2048]{1,0:T(8,128)(2,1)S(1)} %get-tuple-element.27.x_ref, s32[16,256]{1,0:T(8,128)S(1)} %get-tuple-element.29.refs_3_.k_ref, ...), custom_call_target="tpu_custom_call" | custom-call | flops 20000000000 | bytes 4194304 | tf_op jit(solution)/shard_map/high_side_decode/pallas_call | solution.py:419
  30.1 0.1 collective-permute-start.2
  30.1 0.8 %copy.30 = bf16[2,2048,84]{1,0,2:T(2,128)(2,1)} copy(bf16[2,2048,84]{1,0,2:T(2,128)(2,1)S(1)} %bitcast.16) | data formatting | bytes 1376256
  31.0 0.8 %collective-permute-done.2.other_ref = bf16[84,2048]{1,0:T(8,128)(2,1)S(1)} collective-permute-done((bf16[84,2048]{1,0:T(8,128)(2,1)S(1)}, bf16[84,2048]{1,0:T(8,128)(2,1)S(1)}, u32[]{:S(2)}, u32[]{:S(2)}) %collective-permute-start.2) | collective-permute-done | bytes 344096 | tf_op jit(solution)/shard_map/ppermute | solution.py:578
  31.8 0.0 copy-done
  31.8 0.0 copy-done.1
  31.8 1.0 %week.1 = f32[84,2048]{1,0:T(8,128)} custom-call(bf16[84,2048]{1,0:T(8,128)(2,1)S(1)} %get-tuple-element.49.total_ref, bf16[84,2048]{1,0:T(8,128)(2,1)S(1)} %collective-permute-done.2.other_ref, f32[84,2048]{1,0:T(8,128)S(1)} %bitcast.17, bf16[84,2048]{1,0:T(8,128)(2,1)S(1)} %bitcast.18), custom_call_target="tpu_custom_call" | custom-call | flops 1000000 | bytes 4194304 | tf_op jit(solution)/shard_map/week/pallas_call | solution.py:419
Async XLA Ops:
  0.6 4.4 %copy-start.8 = (bf16[84,512]{1,0:T(8,128)(2,1)S(1)}, bf16[84,512]{1,0:T(8,128)(2,1)}, u32[]{:S(2)}) copy-start(bf16[84,512]{1,0:T(8,128)(2,1)} %w_embed.3) | copy-start | bytes 258052
  0.6 4.4 %copy-start.11 = (f32[512]{0:T(512)S(1)}, f32[512]{0:T(512)}, u32[]{:S(2)}) copy-start(f32[512]{0:T(512)} %param.22) | copy-start | bytes 6148
  2.1 13.3 %collective-permute-start.1 = (bf16[176,640]{1,0:T(8,128)(2,1)S(1)}, bf16[176,640]{1,0:T(8,128)(2,1)S(1)}, u32[]{:S(2)}, u32[]{:S(2)}) collective-permute-start(bf16[176,640]{1,0:T(8,128)(2,1)S(1)} %get-tuple-element.43), channel_id=1, source_target_pairs={{0,2},{2,4},{4,6},{6,8},{8,10},{10,12},{12,14},{14,0},{1,3},{3,5},... | collective-permute-start | bytes 675848 | tf_op jit(solution)/shard_map/ppermute | solution.py:485
  5.1 3.3 %copy-start.2 = (bf16[512,512]{1,0:T(8,128)(2,1)S(1)}, bf16[512,512]{1,0:T(8,128)(2,1)}, u32[]{:S(2)}) copy-start(bf16[512,512]{1,0:T(8,128)(2,1)} %refs_4_.1) | copy-start | bytes 1572868
  5.1 3.3 %copy-start.3 = (bf16[512,512]{1,0:T(8,128)(2,1)S(1)}, bf16[512,512]{1,0:T(8,128)(2,1)}, u32[]{:S(2)}) copy-start(bf16[512,512]{1,0:T(8,128)(2,1)} %refs_5_.1) | copy-start | bytes 1572868
  5.1 3.3 %copy-start.4 = (bf16[512,512]{1,0:T(8,128)(2,1)S(1)}, bf16[512,512]{1,0:T(8,128)(2,1)}, u32[]{:S(2)}) copy-start(bf16[512,512]{1,0:T(8,128)(2,1)} %refs_8_.1) | copy-start | bytes 1572868
  5.1 3.3 %copy-start.5 = (bf16[512,512]{1,0:T(8,128)(2,1)S(1)}, bf16[512,512]{1,0:T(8,128)(2,1)}, u32[]{:S(2)}) copy-start(bf16[512,512]{1,0:T(8,128)(2,1)} %refs_9_.1) | copy-start | bytes 1572868
  5.1 3.3 %copy-start.6 = (bf16[512,512]{1,0:T(8,128)(2,1)S(1)}, bf16[512,512]{1,0:T(8,128)(2,1)}, u32[]{:S(2)}) copy-start(bf16[512,512]{1,0:T(8,128)(2,1)} %refs_11_.1) | copy-start | bytes 1572868
  5.1 3.3 %copy-start.7 = (bf16[512,512]{1,0:T(8,128)(2,1)S(1)}, bf16[512,512]{1,0:T(8,128)(2,1)}, u32[]{:S(2)}) copy-start(bf16[512,512]{1,0:T(8,128)(2,1)} %refs_12_.1) | copy-start | bytes 1572868
  5.1 3.2 %copy-start.9 = (bf16[512,84]{0,1:T(8,128)(2,1)S(1)}, bf16[512,84]{0,1:T(8,128)(2,1)}, u32[]{:S(2)}) copy-start(bf16[512,84]{0,1:T(8,128)(2,1)} %param.33) | copy-start | bytes 258052
  5.1 3.2 %copy-start.12 = (f32[512]{0:T(512)S(1)}, f32[512]{0:T(512)}, u32[]{:S(2)}) copy-start(f32[512]{0:T(512)} %param.24) | copy-start | bytes 6148
  5.1 3.2 %copy-start.13 = (f32[512]{0:T(512)S(1)}, f32[512]{0:T(512)}, u32[]{:S(2)}) copy-start(f32[512]{0:T(512)} %param.25) | copy-start | bytes 6148
  5.2 3.2 %copy-start.14 = (f32[512]{0:T(512)S(1)}, f32[512]{0:T(512)}, u32[]{:S(2)}) copy-start(f32[512]{0:T(512)} %param.28) | copy-start | bytes 6148
  5.2 3.2 %copy-start.15 = (f32[512]{0:T(512)S(1)}, f32[512]{0:T(512)}, u32[]{:S(2)}) copy-start(f32[512]{0:T(512)} %param.32) | copy-start | bytes 6148
  6.9 12.1 %collective-permute-start = (bf16[176,640]{1,0:T(8,128)(2,1)S(1)}, bf16[176,640]{1,0:T(8,128)(2,1)S(1)}, u32[]{:S(2)}, u32[]{:S(2)}) collective-permute-start(bf16[176,640]{1,0:T(8,128)(2,1)S(1)} %get-tuple-element.28), channel_id=1, source_target_pairs={{2,0},{4,2},{6,4},{8,6},{10,8},{12,10},{14,12},{0,14},{3,1},{5,3},... | collective-permute-start | bytes 675848 | tf_op jit(solution)/shard_map/ppermute | solution.py:503
  15.4 3.7 %copy-start.10 = (s32[2048,3]{0,1:T(4,128)S(1)}, s32[2048,3]{0,1:T(4,128)}, u32[]{:S(2)}) copy-start(s32[2048,3]{0,1:T(4,128)} %param.36) | copy-start | bytes 73732
  15.4 3.7 %copy-start.16 = (f32[84]{0:T(128)S(1)}, f32[84]{0:T(128)}, u32[]{:S(2)}) copy-start(f32[84]{0:T(128)} %param.34) | copy-start | bytes 1012
  19.1 12.7 %copy-start = (f32[2048,84]{0,1:T(8,128)S(1)}, f32[2048,84]{0,1:T(8,128)}, u32[]{:S(2)}) copy-start(f32[2048,84]{0,1:T(8,128)} %param.39) | copy-start | bytes 2064388
  19.1 12.7 %copy-start.1 = (bf16[2048,84]{0,1:T(8,128)(2,1)S(1)}, bf16[2048,84]{0,1:T(8,128)(2,1)}, u32[]{:S(2)}) copy-start(bf16[2048,84]{0,1:T(8,128)(2,1)} %param.38) | copy-start | bytes 1032196
  30.1 1.7 %collective-permute-start.2 = (bf16[84,2048]{1,0:T(8,128)(2,1)S(1)}, bf16[84,2048]{1,0:T(8,128)(2,1)S(1)}, u32[]{:S(2)}, u32[]{:S(2)}) collective-permute-start(bf16[84,2048]{1,0:T(8,128)(2,1)S(1)} %get-tuple-element.49.total_ref), channel_id=1, source_target_pairs={{0,1},{1,0},{2,3},{3,2},{4,5},{5,4},{6,7},{7,6},{8,9},{9,8},{10,11... | collective-permute-start | bytes 1032200 | tf_op jit(solution)/shard_map/ppermute | solution.py:578
